TPU v7x, 32 devices: a whole 2x2x4 slice. The times are simulated.
32 devices in a mesh: pairs: 8 (over z, y), aux: 4 (over x, core).
Axes of the slice: x: 2, y: 2, z: 4, core: 2. Of those that a mesh axis runs over, the one named last changes fastest.
Arguments:
- cholesky_slab: bfloat16 [2048, 35840], P('pairs', 'aux'), may hold values from -40 to 40, as said below
- test_matrix: bfloat16 [35840, 768], P('aux', 'pairs'), may hold values from -0.03125 to 0.03125
Outputs:
- projected: float32 [768, 35840], P('pairs', 'aux')
Inputs may be any that keep to these rules, and one draw needn't show every extreme that they name: cholesky_slab: real entries with varying row and column magnitudes.
All inputs are finite; a program needn't handle non-finite values.
Results may differ from a plain program's by a relative error of at most 0.0003.
Values may be sent and summed in bfloat16 or wider, within the bound.
No kernel may reach another device: no remote copies, remote signals or barrier semaphores. Data moves between devices by JAX's collectives and lax.ppermute only.
A program may use at most 128 MiB of HBM per device.

v0:
```python
import jax
import jax.numpy as jnp
from jax import lax
from jax.sharding import PartitionSpec as P


def gram_local(sketch_part):
    return jnp.dot(
        sketch_part.T,
        sketch_part,
        precision=lax.Precision.HIGHEST,
        preferred_element_type=jnp.float32,
    )


def basis_from(gram_matrix, sketch_part):
    lower_factor = jnp.linalg.cholesky(gram_matrix)
    return jax.scipy.linalg.solve_triangular(lower_factor, sketch_part.T, lower=True)


def body(cholesky_slab, test_matrix):
    partial_value = jnp.dot(
        cholesky_slab,
        lax.all_gather(test_matrix, "pairs", axis=1, tiled=True),
        preferred_element_type=jnp.float32,
    )
    sketch = lax.psum(partial_value, "aux")
    gram_matrix = lax.psum(gram_local(sketch), "pairs")
    basis_full = basis_from(gram_matrix, sketch)
    return lax.psum_scatter(
        jnp.dot(
            basis_full,
            cholesky_slab,
            precision=lax.Precision.HIGHEST,
            preferred_element_type=jnp.float32,
        ),
        "pairs",
        scatter_dimension=0,
        tiled=True,
    )


def solution(mesh):
    in_specs = (P("pairs", "aux"), P("aux", "pairs"))
    out_specs = P("pairs", "aux")
    return jax.shard_map(body, mesh=mesh, in_specs=in_specs, out_specs=out_specs, check_vma=False)
```

profile of v0, /device:TPU:0, one launch (start us, length us, event | category | flops | bytes accessed | tf_op | source)
XLA Modules:
  0.0 1054.1 jit_solution(14208989793829400956)
XLA Ops:
  6.5 0.7 all-gather.2.cloned.1.call-update
  7.3 195.8 %all-gather.2.cloned.1.call-done = bf16[8960,768]{0,1:T(8,128)(2,1)} async-done(((bf16[8960,96]{0,1:T(8,128)(2,1)}), bf16[8960,768]{0,1:T(8,128)(2,1)}) %all-gather.2.cloned.1.call-update) | async-done | bytes 13762576 | tf_op jit(solution)/shard_map/all_gather | solution.py:24
  203.1 10.9 %fusion.50 = f32[256,768]{1,0:T(8,128)} fusion(bf16[256,8960]{1,0:T(8,128)(2,1)} %param.2, bf16[8960,768]{0,1:T(8,128)(2,1)} %all-gather.2.cloned.1.call-done), kind=kOutput, calls=%fused_computation.112 | convolution fusion | flops 3523215360 | bytes 19136512 | tf_op jit(solution)/shard_map/dot_general | solution.py:22
  214.1 32.9 %all-reduce.4.cloned.1.call-done = f32[256,768]{1,0:T(8,128)} async-done(((f32[256,768]{1,0:T(8,128)}), f32[256,768]{1,0:T(8,128)}) %all-reduce.4.cloned.1.call-update) | async-done | bytes 786448 | tf_op jit(solution)/shard_map/psum | solution.py:27
  247.0 4.9 fusion.51
  252.0 108.8 %all-reduce.6.cloned.1.call-done = f32[768,768]{0,1:T(8,128)} async-done(((f32[768,768]{0,1:T(8,128)}), f32[768,768]{0,1:T(8,128)}) %all-reduce.6.cloned.1.call-update) | async-done | bytes 2359312 | tf_op jit(solution)/shard_map/psum | solution.py:28
  360.8 3.7 copy.4
  364.5 2.0 fusion
  366.5 1.4 copy-done.2
  367.9 11.7 %cholesky.165 = f32[128,128]{1,0:T(8,128)S(1)} custom-call(f32[128,128]{1,0:T(8,128)S(1)} %cholesky.424), custom_call_target="Cholesky" | custom-call | tf_op jit(solution)/shard_map/jit(cholesky)/cholesky | solution.py:17
  379.6 9.8 custom-call.47
  389.6 1.4 constant_dynamic-update-slice_fusion.15
  391.0 1.4 convolution_subtract_fusion
  392.4 11.7 %cholesky.188 = f32[128,128]{1,0:T(8,128)S(1)} custom-call(f32[128,128]{1,0:T(8,128)S(1)} %cholesky.428), custom_call_target="Cholesky" | custom-call | tf_op jit(solution)/shard_map/jit(cholesky)/cholesky | solution.py:17
  404.2 9.9 custom-call.48
  414.5 1.5 convolution_subtract_fusion.1
  416.1 11.7 %cholesky.354 = f32[128,128]{1,0:T(8,128)S(1)} custom-call(f32[128,128]{1,0:T(8,128)S(1)} %cholesky.433), custom_call_target="Cholesky" | custom-call | tf_op jit(solution)/shard_map/jit(cholesky)/cholesky | solution.py:17
  427.8 0.7 compare_reduce_fusion.3
  428.5 9.8 custom-call.49
  438.7 1.6 convolution_subtract_fusion.2
  440.2 11.9 %cholesky.373 = f32[128,128]{1,0:T(8,128)S(1)} custom-call(f32[128,128]{1,0:T(8,128)S(1)} %cholesky.438), custom_call_target="Cholesky" | custom-call | tf_op jit(solution)/shard_map/jit(cholesky)/cholesky | solution.py:17
  452.2 0.6 compare_reduce_fusion.2
  452.8 9.8 custom-call.50
  462.9 1.5 convolution_subtract_fusion.7
  464.4 11.7 %cholesky.392 = f32[128,128]{1,0:T(8,128)S(1)} custom-call(f32[128,128]{1,0:T(8,128)S(1)} %cholesky.443), custom_call_target="Cholesky" | custom-call | tf_op jit(solution)/shard_map/jit(cholesky)/cholesky | solution.py:17
  476.1 0.7 compare_reduce_fusion.1
  476.8 9.8 custom-call.51
  486.8 1.3 convolution_subtract_fusion.9
  488.2 12.1 %cholesky.410 = f32[128,128]{1,0:T(8,128)S(1)} custom-call(f32[128,128]{1,0:T(8,128)S(1)} %convolution_subtract_fusion.9), custom_call_target="Cholesky" | custom-call | tf_op jit(solution)/shard_map/jit(cholesky)/cholesky | solution.py:17
  500.3 0.7 compare_reduce_fusion
  501.0 0.7 compare_reduce_fusion.4
  505.5 1.6 select_select_fusion
  507.0 17.6 %while.1 = (s32[]{:T(128)}, f32[768,768]{1,0:T(8,128)}, s32[6,2]{0,1:T(2,128)S(1)}, f32[6,128,128]{2,1,0:T(8,128)S(1)}, s32[]{:T(128)}) while((s32[]{:T(128)}, f32[768,768]{1,0:T(8,128)}, s32[6,2]{0,1:T(2,128)S(1)}, f32[6,128,128]{2,1,0:T(8,128)S(1)}, s32[]{:T(128)}) %tuple.40), condition=%wide.while_cond, body=%wide.while_body.sunk | while | flops 2 | bytes 131189 | solution.py:18
  507.7 2.2 bitcast_dynamic-update-slice_fusion.2
  510.1 0.6 fusion.68
  510.7 2.2 bitcast_dynamic-update-slice_fusion.2
  513.6 2.2 bitcast_dynamic-update-slice_fusion.2
  516.5 2.2 bitcast_dynamic-update-slice_fusion.2
  519.5 2.2 bitcast_dynamic-update-slice_fusion.2
  522.4 2.2 bitcast_dynamic-update-slice_fusion.2
  524.6 59.0 %custom-call.52 = f32[6,128,128]{1,2,0:T(8,128)S(1)} custom-call(f32[6,128,128]{2,1,0:T(8,128)S(1)} %get-tuple-element.12), custom_call_target="InvertDiagBlocksLowerTriangular" | custom-call | tf_op jit(solution)/shard_map/jit(_solve_triangular)/triangular_solve | solution.py:18
  583.9 1.2 convolution_subtract_fusion.8
  585.5 1.5 convolution_subtract_fusion.6
  587.3 1.8 convolution_subtract_fusion.5
  589.4 1.9 convolution_subtract_fusion.4
  591.7 2.2 convolution_subtract_fusion.3
  594.2 16.7 %fusion.52 = f32[768,8960]{1,0:T(8,128)} fusion(f32[768,256]{1,0:T(8,128)S(1)} %convolution_dynamic-update-slice_fusion.2, bf16[256,8960]{1,0:T(8,128)(2,1)} %param.2), kind=kOutput, calls=%fused_computation.114 | convolution fusion | flops 21139292160 | bytes 32899072 | tf_op jit(solution)/shard_map/dot_general | solution.py:31
  611.0 436.4 %reduce-scatter.2.cloned.1.call-done = f32[96,8960]{1,0:T(8,128)} async-done(((f32[768,8960]{1,0:T(8,128)}), f32[96,8960]{1,0:T(8,128)}) %reduce-scatter.2.cloned.1.call-update) | async-done | bytes 3440656 | tf_op jit(solution)/shard_map/reduce_scatter | solution.py:30
  (48 shorter events, 7.1 us)
Async XLA Ops:
  6.5 196.6 %all-gather.2.cloned.1.call-start = ((), (), s32[]{:S(2)}) async-start(), calls=%async_computation.1 | async-start | bytes 15482880 | tf_op jit(solution)/shard_map/all_gather | solution.py:24
  7.3 239.8 %all-reduce.4.cloned.1.call-start = ((), (), s32[]{:S(2)}) async-start(), calls=%async_computation.2 | async-start | bytes 1572864 | tf_op jit(solution)/shard_map/psum | solution.py:27
  214.1 146.7 %all-reduce.6.cloned.1.call-start = ((), (), s32[]{:S(2)}) async-start(), calls=%async_computation.3 | async-start | bytes 4718592 | tf_op jit(solution)/shard_map/psum | solution.py:28
  251.9 795.5 %reduce-scatter.2.cloned.1.call-start = ((), (), s32[]{:S(2)}) async-start(), calls=%async_computation.4 | async-start | bytes 30965760 | tf_op jit(solution)/shard_map/reduce_scatter | solution.py:30
  360.8 3.7 copy-start
  366.5 1.4 copy-start.2
  505.4 78.1 %copy-start.1 = (f32[256,768]{1,0:T(8,128)S(1)}, f32[256,768]{1,0:T(8,128)}, u32[]{:S(2)}) copy-start(f32[256,768]{1,0:T(8,128)} %all-reduce.4.cloned.1.call-done) | copy-start | bytes 2359300
Sparse Core Ops, SparseCore 0:
  9.5 193.5 all-gather.1
  214.2 32.7 all-reduce.3
  252.0 108.7 all-reduce.5
  611.1 436.1 reduce-scatter.1
where the time goes:
time: 1060 us; the launch traced here: 1050 us
  waiting for transfers between devices  775 us (73%)
  other arithmetic  186 us (18%)
  matrix products  52.9 us (5%)
  local copies, waits for them, and re-layouts  22.8 us (2%)
  between operations  17.4 us (2%)
    reduce_scatter x1, waiting for transfers between devices, body(): lax.psum_scatter(jnp.dot(basis_full, cholesky_slab, precision=lax.Precisi...  436 us
    all_gather x1, waiting for transfers between devices, body(): lax.all_gather(test_matrix, 'pairs', axis=1, tiled=True)  196 us
    another operation x22, other arithmetic, basis_from(): lower_factor = jnp.linalg.cholesky(gram_matrix)  124 us
    psum x1, waiting for transfers between devices, body(): gram_matrix = lax.psum(gram_local(sketch), 'pairs')  109 us
    another operation x3, other arithmetic, basis_from(): jax.scipy.linalg.solve_triangular(lower_factor, sketch_part.T, lower=True)  60.5 us
    psum x1, waiting for transfers between devices, body(): sketch = lax.psum(partial_value, 'aux')  32.9 us
  transfers between devices with their start and end apart: 4, of which 4 were waited for; matrix products, arithmetic and copies ran while one was open for 0% of the time, Pallas kernels for 0%

commit v1 on v0

v1 whole, which is shorter than its diff:
```python
import jax
import jax.numpy as jnp
from jax import lax
from jax.sharding import PartitionSpec as P

HIGHEST = lax.Precision.HIGHEST


def split3(x):
    hi = lax.reduce_precision(x, 8, 7)
    rest = x - hi
    mid = lax.reduce_precision(rest, 8, 7)
    return tuple(part.astype(jnp.bfloat16) for part in (hi, mid, rest - mid))


def dot_t(a, b):
    return lax.dot_general(a, b, (((0,), (0,)), ((), ())), preferred_element_type=jnp.float32)


def body(slab, test_matrix):
    n_pairs = lax.axis_size("pairs")
    slab_cols = lax.all_to_all(slab, "pairs", split_axis=1, concat_axis=0, tiled=True)
    test_rows = lax.all_to_all(test_matrix, "pairs", split_axis=0, concat_axis=1, tiled=True)
    largest = lax.pmax(jnp.max(jnp.abs(slab)).astype(jnp.float32), ("pairs", "aux"))

    partial_value = jnp.dot(slab_cols, test_rows, preferred_element_type=jnp.float32)
    rows = lax.psum_scatter(partial_value, ("pairs", "aux"), scatter_dimension=0, tiled=True)
    sketch = lax.all_gather(rows, ("pairs", "aux"), axis=0, tiled=True)

    gram = lax.dot_general(sketch, sketch, (((0,), (0,)), ((), ())), precision=HIGHEST, preferred_element_type=jnp.float32)
    hi, mid, lo = split3(sketch)
    weighted = dot_t(lo, slab_cols) + dot_t(mid, slab_cols) + dot_t(hi, slab_cols)

    factor = jnp.linalg.cholesky(gram)
    projected = jax.scipy.linalg.solve_triangular(factor, weighted, lower=True)

    all_rows = slab_cols.shape[0]
    bound = jnp.maximum(largest, 1e-30) * (all_rows ** 0.5)
    scale = 16384.0 / bound
    sent = (projected * scale).astype(jnp.float16)
    got = lax.all_to_all(sent, "pairs", split_axis=0, concat_axis=1, tiled=True)
    return got.astype(jnp.float32) * (bound / 16384.0)


def solution(mesh):
    in_specs = (P("pairs", "aux"), P("aux", "pairs"))
    out_specs = P("pairs", "aux")
    return jax.shard_map(body, mesh=mesh, in_specs=in_specs, out_specs=out_specs, check_vma=False)
```

time: 1060 us -> 712 us (0.67)
  waiting for transfers between devices: 775 us -> 314 us
  blocking collectives: 0 us -> 40.6 us
  local copies, waits for them, and re-layouts: 22.8 us -> 50.8 us
  matrix products: 52.9 us -> 76.4 us
  starting transfers between devices: 0.12 us -> 15.1 us
    reduce_scatter x1, waiting for transfers between devices: 436 us -> 114 us  [body(): lax.psum_scatter(partial_value, ('pairs', 'aux'), scatter_dimension=0, ti...]
    all_to_all x0 -> x3, waiting for transfers between devices: none -> 173 us  [the longest x1 97.1 us: body(): lax.all_to_all(slab, 'pairs', split_axis=1, concat_axis=0, tiled=True)]
    all_gather x1, waiting for transfers between devices: 196 us -> 27.4 us  [body(): sketch = lax.all_gather(rows, ('pairs', 'aux'), axis=0, tiled=True)]
    psum x2 -> x0, waiting for transfers between devices: 142 us -> none  [the longest x1 109 us: body(): gram_matrix = lax.psum(gram_local(sketch), 'pairs')]
    pmax x0 -> x1, blocking collectives: none -> 40.6 us  [body(): lax.pmax(jnp.max(jnp.abs(slab)).astype(jnp.float32), ('pairs', 'aux'))]
    dot_general x3 -> x5, matrix products: 32.5 us -> 50 us  [the longest x3 21.3 us: dot_t(): lax.dot_general(a, b, (((0,), (0,)), ((), ())), preferred_element_type=jn...]
    all_to_all x0 -> x3, starting transfers between devices: none -> 15.1 us  [the longest x1 7.41 us: body(): lax.all_to_all(slab, 'pairs', split_axis=1, concat_axis=0, tiled=True)]
    all_to_all x0 -> x3, local copies, waits for them, and re-layouts: none -> 11.3 us  [the longest x1 6.68 us: body(): lax.all_to_all(slab, 'pairs', split_axis=1, concat_axis=0, tiled=True)]
  transfers between devices with their start and end apart: 4 -> 5, of which waited for: 4 -> 5; matrix products, arithmetic and copies ran while one was open for 0% -> 2% of each run, Pallas kernels for 0% -> 0%
where the time goes in v1:
time: 712 us; the launch traced here: 707 us
  waiting for transfers between devices  314 us (44%)
  other arithmetic  191 us (27%)
  matrix products  76.4 us (11%)
  local copies, waits for them, and re-layouts  50.8 us (7%)
  blocking collectives  40.6 us (6%)
  between operations  18.7 us (3%)
  starting transfers between devices  15.1 us (2%)
    another operation x22, other arithmetic, body(): factor = jnp.linalg.cholesky(gram)  124 us
    reduce_scatter x1, waiting for transfers between devices, body(): lax.psum_scatter(partial_value, ('pairs', 'aux'), scatter_dimension=0, ti...  114 us
    all_to_all x1, waiting for transfers between devices, body(): lax.all_to_all(slab, 'pairs', split_axis=1, concat_axis=0, tiled=True)  97.1 us
    another operation x3, other arithmetic, body(): projected = jax.scipy.linalg.solve_triangular(factor, weighted, lower=True)  61.3 us
    all_to_all x1, waiting for transfers between devices, body(): got = lax.all_to_all(sent, 'pairs', split_axis=0, concat_axis=1, tiled=True)  41.6 us
    pmax x1, blocking collectives, body(): lax.pmax(jnp.max(jnp.abs(slab)).astype(jnp.float32), ('pairs', 'aux'))  40.6 us
    all_to_all x1, waiting for transfers between devices, body(): lax.all_to_all(test_matrix, 'pairs', split_axis=0, concat_axis=1, tiled=T...  34.7 us
    all_gather x1, waiting for transfers between devices, body(): sketch = lax.all_gather(rows, ('pairs', 'aux'), axis=0, tiled=True)  27.4 us
  transfers between devices with their start and end apart: 5, of which 5 were waited for; matrix products, arithmetic and copies ran while one was open for 2% of the time, Pallas kernels for 0%

profile of v1, /device:TPU:0, one launch (start us, length us, event | category | flops | bytes accessed | tf_op | source)
XLA Modules:
  0.0 707.1 jit_solution(12942498475199214760)
XLA Ops:
  6.5 6.6 copy.10
  13.1 7.4 %all-to-all-start = ((bf16[256,8,1120]{0,2,1:T(8,128)(2,1)}), bf16[256,8,1120]{0,2,1:T(8,128)(2,1)}, u32[]{:S(2)}, u32[]{:S(2)}) async-start(bf16[256,8,1120]{0,2,1:T(8,128)(2,1)} %bitcast.95), calls=%async_computation | async-start | bytes 9175040 | tf_op jit(solution)/shard_map/all_to_all | solution.py:22
  20.6 3.2 all_to_all.40
  25.2 97.1 %all-to-all-done = bf16[256,8,1120]{0,2,1:T(8,128)(2,1)} async-done(((bf16[256,8,1120]{0,2,1:T(8,128)(2,1)}), bf16[256,8,1120]{0,2,1:T(8,128)(2,1)}, u32[]{:S(2)}, u32[]{:S(2)}) %all-to-all-start) | async-done | bytes 4587552 | tf_op jit(solution)/shard_map/all_to_all | solution.py:22
  122.3 3.6 all-to-all-start.1
  125.9 6.7 copy.11
  132.6 34.7 %all-to-all-done.1 = bf16[8,1120,96]{1,2,0:T(8,128)(2,1)S(1)} async-done(((bf16[8,1120,96]{1,2,0:T(8,128)(2,1)}), bf16[8,1120,96]{1,2,0:T(8,128)(2,1)S(1)}, u32[]{:S(2)}, u32[]{:S(2)}) %all-to-all-start.1) | async-done | bytes 1720352 | tf_op jit(solution)/shard_map/all_to_all | solution.py:23
  167.3 8.4 %fusion.53 = f32[2048,768]{1,0:T(8,128)} fusion(bf16[2048,1120]{1,0:T(8,128)(2,1)} %bitcast.96, bf16[1120,768]{0,1:T(8,128)(2,1)S(1)} %bitcast.102), kind=kOutput, calls=%fused_computation.123 | convolution fusion | flops 3523215360 | bytes 12599296 | tf_op jit(solution)/shard_map/dot_general | solution.py:26
  175.8 113.5 %reduce-scatter.2.cloned.1.call-done = f32[64,768]{1,0:T(8,128)} async-done(((f32[2048,768]{1,0:T(8,128)}), f32[64,768]{1,0:T(8,128)}) %reduce-scatter.2.cloned.1.call-update) | async-done | bytes 196624 | tf_op jit(solution)/shard_map/reduce_scatter | solution.py:27
  289.3 3.5 abs_reduce_fusion
  292.8 40.6 %pmax.7 = f32[]{:T(128)} all-reduce(bf16[]{:T(256)} %abs_reduce_fusion), channel_id=1, replica_groups=mesh['pairs'=8,'aux'=4] {'pairs','aux'}, use_global_device_ids=true, to_apply=%region_14.15 | all-reduce | flops 1 | bytes 6 | tf_op jit(solution)/shard_map/pmax | solution.py:24
  334.1 27.4 %all-gather.2.cloned.1.call-done = f32[2048,768]{1,0:T(8,128)} async-done(((f32[64,768]{1,0:T(8,128)}), f32[2048,768]{1,0:T(8,128)}) %all-gather.2.cloned.1.call-update) | async-done | bytes 6291472 | tf_op jit(solution)/shard_map/all_gather | solution.py:28
  361.4 20.3 %fusion.54 = f32[768,768]{1,0:T(8,128)S(1)} fusion(f32[2048,768]{1,0:T(8,128)} %all-gather.2.cloned.1.call-done), kind=kOutput, calls=%fused_computation.124 | convolution fusion | flops 14495514624 | bytes 8650752 | tf_op jit(solution)/shard_map/dot_general | solution.py:30
  381.8 2.3 copy.13
  384.1 2.0 fusion.3
  387.5 11.7 %cholesky.165 = f32[128,128]{1,0:T(8,128)S(1)} custom-call(f32[128,128]{1,0:T(8,128)S(1)} %cholesky.424), custom_call_target="Cholesky" | custom-call | tf_op jit(solution)/shard_map/jit(cholesky)/cholesky | solution.py:34
  399.2 9.8 %custom-call.47 = f32[1,128,128]{1,2,0:T(8,128)S(1)} custom-call(f32[1,128,128]{2,1,0:T(8,128)S(1)} %get-tuple-element.48), custom_call_target="InvertDiagBlocksLowerTriangular" | custom-call | tf_op jit(solution)/shard_map/jit(cholesky)/cholesky | solution.py:34
  412.0 11.7 %cholesky.188 = f32[128,128]{1,0:T(8,128)S(1)} custom-call(f32[128,128]{1,0:T(8,128)S(1)} %cholesky.428), custom_call_target="Cholesky" | custom-call | tf_op jit(solution)/shard_map/jit(cholesky)/cholesky | solution.py:34
  423.8 10.0 %custom-call.48 = f32[1,128,128]{1,2,0:T(8,128)S(1)} custom-call(f32[1,128,128]{2,1,0:T(8,128)S(1)} %get-tuple-element.45), custom_call_target="InvertDiagBlocksLowerTriangular" | custom-call | tf_op jit(solution)/shard_map/jit(cholesky)/cholesky | solution.py:34
  435.7 11.7 %cholesky.354 = f32[128,128]{1,0:T(8,128)S(1)} custom-call(f32[128,128]{1,0:T(8,128)S(1)} %cholesky.433), custom_call_target="Cholesky" | custom-call | tf_op jit(solution)/shard_map/jit(cholesky)/cholesky | solution.py:34
  448.1 9.8 %custom-call.49 = f32[1,128,128]{1,2,0:T(8,128)S(1)} custom-call(f32[1,128,128]{2,1,0:T(8,128)S(1)} %get-tuple-element.42), custom_call_target="InvertDiagBlocksLowerTriangular" | custom-call | tf_op jit(solution)/shard_map/jit(cholesky)/cholesky | solution.py:34
  458.3 1.6 convolution_subtract_fusion.7
  459.8 12.1 %cholesky.373 = f32[128,128]{1,0:T(8,128)S(1)} custom-call(f32[128,128]{1,0:T(8,128)S(1)} %cholesky.438), custom_call_target="Cholesky" | custom-call | tf_op jit(solution)/shard_map/jit(cholesky)/cholesky | solution.py:34
  472.7 9.8 %custom-call.50 = f32[1,128,128]{1,2,0:T(8,128)S(1)} custom-call(f32[1,128,128]{2,1,0:T(8,128)S(1)} %get-tuple-element.39), custom_call_target="InvertDiagBlocksLowerTriangular" | custom-call | tf_op jit(solution)/shard_map/jit(cholesky)/cholesky | solution.py:34
  484.2 11.7 %cholesky.392 = f32[128,128]{1,0:T(8,128)S(1)} custom-call(f32[128,128]{1,0:T(8,128)S(1)} %cholesky.443), custom_call_target="Cholesky" | custom-call | tf_op jit(solution)/shard_map/jit(cholesky)/cholesky | solution.py:34
  496.7 9.8 %custom-call.51 = f32[1,128,128]{1,2,0:T(8,128)S(1)} custom-call(f32[1,128,128]{2,1,0:T(8,128)S(1)} %get-tuple-element.36), custom_call_target="InvertDiagBlocksLowerTriangular" | custom-call | tf_op jit(solution)/shard_map/jit(cholesky)/cholesky | solution.py:34
  508.0 11.9 %cholesky.410 = f32[128,128]{1,0:T(8,128)S(1)} custom-call(f32[128,128]{1,0:T(8,128)S(1)} %convolution_subtract_fusion.9), custom_call_target="Cholesky" | custom-call | tf_op jit(solution)/shard_map/jit(cholesky)/cholesky | solution.py:34
  525.2 1.6 select_select_fusion
  526.8 21.4 %while.1 = (s32[]{:T(128)}, f32[768,768]{1,0:T(8,128)}, s32[6,2]{0,1:T(2,128)S(1)}, f32[6,128,128]{2,1,0:T(8,128)}, s32[]{:T(128)}) while((s32[]{:T(128)}, f32[768,768]{1,0:T(8,128)}, s32[6,2]{0,1:T(2,128)S(1)}, f32[6,128,128]{2,1,0:T(8,128)}, s32[]{:T(128)}) %tuple.40), condition=%wide.while_cond, body=%wide.while_body.sunk | while | flops 2 | bytes 132705 | solution.py:35
  527.5 2.9 bitcast_dynamic-update-slice_fusion.2
  531.1 2.9 bitcast_dynamic-update-slice_fusion.2
  534.7 2.9 bitcast_dynamic-update-slice_fusion.2
  538.2 2.9 bitcast_dynamic-update-slice_fusion.2
  541.8 2.9 bitcast_dynamic-update-slice_fusion.2
  545.4 2.8 bitcast_dynamic-update-slice_fusion.2
  548.3 59.8 %custom-call.52 = f32[6,128,128]{1,2,0:T(8,128)S(1)} custom-call(f32[6,128,128]{2,1,0:T(8,128)} %get-tuple-element.12), custom_call_target="InvertDiagBlocksLowerTriangular" | custom-call | tf_op jit(solution)/shard_map/jit(_solve_triangular)/triangular_solve | solution.py:35
  608.0 8.1 %fusion.1 = f32[768,1120]{0,1:T(8,128)S(1)} fusion(bf16[2048,1120]{1,0:T(8,128)(2,1)} %bitcast.97, f32[2048,768]{1,0:T(8,128)} %all-gather.2.cloned.1.call-done), kind=kOutput, calls=%fused_computation.12 | convolution fusion | flops 3531079680 | bytes 14319616 | tf_op jit(solution)/shard_map/dot_general | solution.py:17
  616.2 6.6 convolution_add_fusion.1
  622.8 6.6 convolution_add_fusion
  632.3 2.0 convolution_subtract_fusion.2
  634.9 2.7 convolution_subtract_fusion.1
  638.2 2.9 convolution_subtract_fusion.3
  641.7 3.7 convolution_subtract_fusion
  646.4 2.7 copy.14
  649.1 4.0 all-to-all-start.2
  653.1 41.6 %all-to-all-done.2 = f16[8,96,1120]{2,1,0:T(8,128)(2,1)S(1)} async-done(((f16[8,96,1120]{2,1,0:T(8,128)(2,1)}), f16[8,96,1120]{2,1,0:T(8,128)(2,1)S(1)}, u32[]{:S(2)}, u32[]{:S(2)}) %all-to-all-start.2) | async-done | bytes 1720352 | tf_op jit(solution)/shard_map/all_to_all | solution.py:41
  695.0 2.1 copy.15
  697.1 2.7 mul.29
  (64 shorter events, 25.0 us)
Async XLA Ops:
  13.1 7.4 %copy-start.1 = (bf16[8960,96]{0,1:T(8,128)(2,1)S(1)}, bf16[8960,96]{0,1:T(8,128)(2,1)}, u32[]{:S(2)}) copy-start(bf16[8960,96]{0,1:T(8,128)(2,1)} %param.3) | copy-start | bytes 5160964
  13.1 109.1 %all-to-all-start = ((bf16[256,8,1120]{0,2,1:T(8,128)(2,1)}), bf16[256,8,1120]{0,2,1:T(8,128)(2,1)}, u32[]{:S(2)}, u32[]{:S(2)}) async-start(bf16[256,8,1120]{0,2,1:T(8,128)(2,1)} %bitcast.95), calls=%async_computation | async-start | bytes 9175040 | tf_op jit(solution)/shard_map/all_to_all | solution.py:22
  122.3 45.0 %all-to-all-start.1 = ((bf16[8,1120,96]{1,2,0:T(8,128)(2,1)}), bf16[8,1120,96]{1,2,0:T(8,128)(2,1)S(1)}, u32[]{:S(2)}, u32[]{:S(2)}) async-start(bf16[8,1120,96]{1,2,0:T(8,128)(2,1)} %copy.12), calls=%async_computation.1 | async-start | bytes 3538944 | tf_op jit(solution)/shard_map/all_to_all | solution.py:23
  125.9 163.4 %reduce-scatter.2.cloned.1.call-start = ((), (), s32[]{:S(2)}) async-start(), calls=%async_computation.4 | async-start | bytes 6488064 | tf_op jit(solution)/shard_map/reduce_scatter | solution.py:27
  175.7 185.7 %all-gather.2.cloned.1.call-start = ((), (), s32[]{:S(2)}) async-start(), calls=%async_computation.5 | async-start | bytes 6488064 | tf_op jit(solution)/shard_map/all_gather | solution.py:28
  386.1 1.4 copy-start
  525.2 91.0 %slice-start = ((s8[4718592]{0:T(1024)(128)(4,1)}), s8[524288]{0:T(1024)(128)(4,1)S(1)}, s32[]{:S(2)}) async-start(s8[4718592]{0:T(1024)(128)(4,1)} %bitcast.98), calls=%async_computation.6 | async-start | bytes 1048576
  608.0 8.2 %slice-start.1 = ((s8[4718592]{0:T(1024)(128)(4,1)}), s8[4194304]{0:T(1024)(128)(4,1)S(1)}, s32[]{:S(2)}) async-start(s8[4718592]{0:T(1024)(128)(4,1)} %bitcast.98), calls=%async_computation.7 | async-start | bytes 8388608
  649.1 45.7 %all-to-all-start.2 = ((f16[8,96,1120]{2,1,0:T(8,128)(2,1)}), f16[8,96,1120]{2,1,0:T(8,128)(2,1)S(1)}, u32[]{:S(2)}, u32[]{:S(2)}) async-start(f16[8,96,1120]{2,1,0:T(8,128)(2,1)} %bitcast.22), calls=%async_computation.3 | async-start | bytes 3538944 | tf_op jit(solution)/shard_map/all_to_all | solution.py:41
Sparse Core Ops, SparseCore 0:
  175.9 113.3 reduce-scatter.1
  292.6 68.7 all-gather.1

commit v2 on v1

--- a/solution.py
+++ b/solution.py
@@ -1,6 +1,8 @@
 import jax
 import jax.numpy as jnp
 from jax import lax
+from jax.experimental import pallas as pl
+from jax.experimental.pallas import tpu as pltpu
 from jax.sharding import PartitionSpec as P
 
 HIGHEST = lax.Precision.HIGHEST
@@ -17,6 +19,93 @@
     return lax.dot_general(a, b, (((0,), (0,)), ((), ())), preferred_element_type=jnp.float32)
 
 
+def invert_block(block):
+    size = block.shape[0]
+    lane = lax.broadcasted_iota(jnp.int32, (8, size), 1)
+    sub = lax.broadcasted_iota(jnp.int32, (8, size), 0)
+
+    def across(x, column):
+        return jnp.broadcast_to(x[:, column : column + 1], (8, size))
+
+    def down(x, row):
+        return jnp.broadcast_to(x[row : row + 1, :], (8, size))
+
+    slabs = [block[8 * i : 8 * i + 8, :] for i in range(size // 8)]
+    for g in range(size // 8):
+        base = 8 * g
+        own = (lane >= base) & (lane < base + 8)
+        slab = slabs[g]
+        marked = jnp.where(own, jnp.where(lane == sub + base, 1.0, 0.0), slab)
+        cols = [across(slab, base + j) for j in range(8)]
+        d = {(i, j): down(cols[j], i) for j in range(8) for i in range(j, 8)}
+        rows = [down(marked, i) for i in range(8)]
+        m, recip = {}, []
+        for j in range(8):
+            recip.append(1.0 / d[j, j])
+            for i in range(j + 1, 8):
+                m[i, j] = d[i, j] * recip[j]
+            for i in range(j + 1, 8):
+                for k in range(j + 1, i + 1):
+                    d[i, k] = d[i, k] - m[i, j] * d[k, j]
+                rows[i] = rows[i] - m[i, j] * rows[j]
+        solved = [rows[j] * recip[j] for j in range(8)]
+        for j in range(6, -1, -1):
+            for i in range(7, j, -1):
+                solved[j] = solved[j] - m[i, j] * solved[i]
+        for i in range(g + 1, size // 8):
+            total = jnp.where(own, 0.0, slabs[i])
+            for j in range(8):
+                total = total - across(slabs[i], base + j) * solved[j]
+            slabs[i] = total
+        scaled = rows[0] * lax.rsqrt(d[0, 0])
+        for j in range(1, 8):
+            scaled = jnp.where(sub == j, rows[j] * lax.rsqrt(d[j, j]), scaled)
+        slabs[g] = scaled
+    return jnp.concatenate(slabs, axis=0)
+
+
+def inverse_factor_kernel(gram_ref, out_ref, work, strip):
+    size = gram_ref.shape[0]
+    tile = 128
+    work[...] = gram_ref[...]
+    row_in = lax.broadcasted_iota(jnp.int32, (tile, tile), 0)
+    col_in = lax.broadcasted_iota(jnp.int32, (tile, tile), 1)
+    col = lax.broadcasted_iota(jnp.int32, (tile, size), 1)
+
+    def step(k, carry):
+        at = pl.multiple_of(k * tile, tile)
+        here = pl.ds(at, tile)
+        inverse = invert_block(work[here, here])
+        inverse = jnp.where(row_in >= col_in, inverse, 0.0)
+        work[here, here] = jnp.where(row_in == col_in, 1.0, 0.0)
+        strip[...] = jnp.dot(inverse, work[here, :], precision=HIGHEST, preferred_element_type=jnp.float32)
+        strip[:, here] = inverse
+        out_ref[here, :] = jnp.where(col < at + tile, strip[...], 0.0)
+
+        def below(i, carry):
+            there = pl.ds(pl.multiple_of(i * tile, tile), tile)
+            work[there, here] = jnp.zeros((tile, tile), jnp.float32)
+            work[there, :] -= jnp.dot(strip[:, there].T, strip[...], precision=HIGHEST, preferred_element_type=jnp.float32)
+            return carry
+
+        return lax.fori_loop(k + 1, size // tile, below, carry)
+
+    lax.fori_loop(0, size // tile, step, 0)
+
+
+def inverse_factor(gram):
+    size = gram.shape[0]
+    return pl.pallas_call(
+        inverse_factor_kernel,
+        out_shape=jax.ShapeDtypeStruct((size, size), jnp.float32),
+        in_specs=[pl.BlockSpec(memory_space=pltpu.VMEM)],
+        out_specs=pl.BlockSpec(memory_space=pltpu.VMEM),
+        scratch_shapes=[pltpu.VMEM((size, size), jnp.float32), pltpu.VMEM((128, size), jnp.float32)],
+        compiler_params=pltpu.CompilerParams(vmem_limit_bytes=32 * 1024 * 1024),
+        cost_estimate=pl.CostEstimate(flops=60 * size**3, bytes_accessed=8 * size**2, transcendentals=0),
+    )(gram)
+
+
 def body(slab, test_matrix):
     n_pairs = lax.axis_size("pairs")
     slab_cols = lax.all_to_all(slab, "pairs", split_axis=1, concat_axis=0, tiled=True)
@@ -31,8 +120,7 @@
     hi, mid, lo = split3(sketch)
     weighted = dot_t(lo, slab_cols) + dot_t(mid, slab_cols) + dot_t(hi, slab_cols)
 
-    factor = jnp.linalg.cholesky(gram)
-    projected = jax.scipy.linalg.solve_triangular(factor, weighted, lower=True)
+    projected = jnp.dot(inverse_factor(gram), weighted, precision=HIGHEST, preferred_element_type=jnp.float32)
 
     all_rows = slab_cols.shape[0]
     bound = jnp.maximum(largest, 1e-30) * (all_rows ** 0.5)

time: 712 us -> 508 us (0.71)
  other arithmetic: 191 us -> 3.73 us
  Pallas kernels: 0 us -> 41.3 us
  matrix products: 76.4 us -> 48.9 us
  local copies, waits for them, and re-layouts: 50.8 us -> 25.2 us
    another operation x25 -> x0, other arithmetic: 185 us -> none  [the longest x22 124 us: body(): factor = jnp.linalg.cholesky(gram)]
    pallas_call x0 -> x1, Pallas kernels: none -> 41.3 us  [inverse_factor(): pl.pallas_call(inverse_factor_kernel, out_shape=jax.ShapeDtypeStruct((siz...]
    another operation x21 -> x0, matrix products: 26.4 us -> none  [the longest x11 16.6 us: body(): projected = jax.scipy.linalg.solve_triangular(factor, weighted, lower=True)]
    another operation x25 -> x0, local copies, waits for them, and re-layouts: 21.6 us -> none
    dot_general x3, matrix products: 21.3 us -> 11.4 us  [dot_t(): lax.dot_general(a, b, (((0,), (0,)), ((), ())), preferred_element_type=jn...]
    dot_general x0 -> x1, matrix products: none -> 8.79 us  [body(): jnp.dot(inverse_factor(gram), weighted, precision=HIGHEST, preferred_elem...]
where the time goes in v2:
time: 508 us; the launch traced here: 503 us
  waiting for transfers between devices  314 us (62%)
  matrix products  48.9 us (10%)
  Pallas kernels  41.3 us (8%)
  blocking collectives  40.6 us (8%)
  local copies, waits for them, and re-layouts  25.2 us (5%)
  starting transfers between devices  15.1 us (3%)
  between operations  14.4 us (3%)
    reduce_scatter x1, waiting for transfers between devices, body(): lax.psum_scatter(partial_value, ('pairs', 'aux'), scatter_dimension=0, ti...  114 us
    all_to_all x1, waiting for transfers between devices, body(): lax.all_to_all(slab, 'pairs', split_axis=1, concat_axis=0, tiled=True)  97.1 us
    all_to_all x1, waiting for transfers between devices, body(): got = lax.all_to_all(sent, 'pairs', split_axis=0, concat_axis=1, tiled=True)  41.6 us
    pallas_call x1, Pallas kernels, inverse_factor(): pl.pallas_call(inverse_factor_kernel, out_shape=jax.ShapeDtypeStruct((siz...  41.3 us
    pmax x1, blocking collectives, body(): lax.pmax(jnp.max(jnp.abs(slab)).astype(jnp.float32), ('pairs', 'aux'))  40.6 us
    all_to_all x1, waiting for transfers between devices, body(): lax.all_to_all(test_matrix, 'pairs', split_axis=0, concat_axis=1, tiled=T...  34.6 us
    all_gather x1, waiting for transfers between devices, body(): sketch = lax.all_gather(rows, ('pairs', 'aux'), axis=0, tiled=True)  27.3 us
    dot_general x1, matrix products, body(): lax.dot_general(sketch, sketch, (((0,), (0,)), ((), ())), precision=HIGHE...  20.3 us
  transfers between devices with their start and end apart: 5, of which 5 were waited for; matrix products, arithmetic and copies ran while one was open for 2% of the time, Pallas kernels for 0%

profile of v2, /device:TPU:0, one launch (start us, length us, event | category | flops | bytes accessed | tf_op | source)
XLA Modules:
  0.0 503.4 jit_solution(4987166051918809341)
XLA Ops:
  6.5 6.6 %copy.8 = bf16[256,8960]{0,1:T(8,128)(2,1)} copy(bf16[256,8960]{1,0:T(8,128)(2,1)} %param.2) | data formatting | bytes 9175040 | tf_op args[0]
  13.1 0.0 copy-start
  13.1 7.4 %all-to-all-start = ((bf16[256,8,1120]{0,2,1:T(8,128)(2,1)}), bf16[256,8,1120]{0,2,1:T(8,128)(2,1)}, u32[]{:S(2)}, u32[]{:S(2)}) async-start(bf16[256,8,1120]{0,2,1:T(8,128)(2,1)} %bitcast.20), calls=%async_computation | async-start | bytes 9175040 | tf_op jit(solution)/shard_map/all_to_all | solution.py:111
  20.5 0.0 copy-done
  20.6 3.2 all_to_all.42
  23.8 1.4 copy.10
  25.2 97.1 %all-to-all-done = bf16[256,8,1120]{0,2,1:T(8,128)(2,1)} async-done(((bf16[256,8,1120]{0,2,1:T(8,128)(2,1)}), bf16[256,8,1120]{0,2,1:T(8,128)(2,1)}, u32[]{:S(2)}, u32[]{:S(2)}) %all-to-all-start) | async-done | bytes 4587552 | tf_op jit(solution)/shard_map/all_to_all | solution.py:111
  122.3 3.6 all-to-all-start.1
  125.9 0.0 reduce-scatter.2.cloned.1.call-start
  125.9 6.7 %copy.9 = bf16[8,256,1120]{2,1,0:T(8,128)(2,1)} copy(bf16[8,256,1120]{1,2,0:T(8,128)(2,1)} %bitcast.1) | data formatting | bytes 9175040 | tf_op jit(solution)/shard_map/all_to_all | solution.py:111
  132.7 34.6 %all-to-all-done.1 = bf16[8,1120,96]{1,2,0:T(8,128)(2,1)S(1)} async-done(((bf16[8,1120,96]{1,2,0:T(8,128)(2,1)}), bf16[8,1120,96]{1,2,0:T(8,128)(2,1)S(1)}, u32[]{:S(2)}, u32[]{:S(2)}) %all-to-all-start.1) | async-done | bytes 1720352 | tf_op jit(solution)/shard_map/all_to_all | solution.py:112
  167.3 8.5 %fusion.4 = f32[2048,768]{1,0:T(8,128)} fusion(bf16[2048,1120]{1,0:T(8,128)(2,1)} %bitcast.21, bf16[1120,768]{0,1:T(8,128)(2,1)S(1)} %bitcast.27), kind=kOutput, calls=%fused_computation.12 | convolution fusion | flops 3523215360 | bytes 12599296 | tf_op jit(solution)/shard_map/dot_general | solution.py:115
  175.8 0.0 reduce-scatter.2.cloned.1.call-update
  175.8 0.0 all-gather.2.cloned.1.call-start
  175.9 113.5 %reduce-scatter.2.cloned.1.call-done = f32[64,768]{1,0:T(8,128)} async-done(((f32[2048,768]{1,0:T(8,128)}), f32[64,768]{1,0:T(8,128)}) %reduce-scatter.2.cloned.1.call-update) | async-done | bytes 196624 | tf_op jit(solution)/shard_map/reduce_scatter | solution.py:116
  289.4 0.0 all-gather.2.cloned.1.call-update
  289.4 3.5 abs_reduce_fusion
  292.9 40.6 %pmax.7 = f32[]{:T(128)} all-reduce(bf16[]{:T(256)} %abs_reduce_fusion), channel_id=1, replica_groups=mesh['pairs'=8,'aux'=4] {'pairs','aux'}, use_global_device_ids=true, to_apply=%region_2.0 | all-reduce | flops 1 | bytes 6 | tf_op jit(solution)/shard_map/pmax | solution.py:113
  334.1 27.3 %all-gather.2.cloned.1.call-done = f32[2048,768]{1,0:T(8,128)} async-done(((f32[64,768]{1,0:T(8,128)}), f32[2048,768]{1,0:T(8,128)}) %all-gather.2.cloned.1.call-update) | async-done | bytes 6291472 | tf_op jit(solution)/shard_map/all_gather | solution.py:117
  361.4 0.0 slice-start
  361.4 0.0 slice-start.2
  361.4 20.3 %fusion.5.gram_ref = f32[768,768]{1,0:T(8,128)S(1)} fusion(f32[2048,768]{1,0:T(8,128)} %all-gather.2.cloned.1.call-done), kind=kOutput, calls=%fused_computation.13 | convolution fusion | flops 14495514624 | bytes 8650752 | tf_op jit(solution)/shard_map/dot_general | solution.py:119
  381.6 0.0 slice-start.1
  381.7 0.0 slice-start.3
  381.7 41.3 %shard_map.28 = f32[768,768]{1,0:T(8,128)S(1)} custom-call(f32[768,768]{1,0:T(8,128)S(1)} %fusion.5.gram_ref), custom_call_target="tpu_custom_call" | custom-call | flops 27179089920 | bytes 4718592 | tf_op jit(solution)/shard_map/pallas_call | solution.py:98
  423.0 0.0 slice-done
  423.0 0.0 slice-done.2
  423.0 0.0 slice-done.1
  423.0 0.0 slice-done.3
  423.0 3.8 fusion.2
  426.9 3.8 convolution_add_fusion.1
  430.6 3.8 convolution_add_fusion
  434.4 8.8 %fusion.1 = f16[768,1120]{0,1:T(8,128)(2,1)S(1)} fusion(f32[768,768]{1,0:T(8,128)S(1)} %shard_map.28, f32[768,1120]{0,1:T(8,128)S(1)} %convolution_add_fusion, f32[]{:T(128)S(6)} %div.6), kind=kOutput, calls=%fused_computation.10 | convolution fusion | flops 7928954880 | bytes 7520260 | tf_op jit(solution)/shard_map/dot_general | solution.py:123
  443.2 2.5 copy.11
  445.7 4.0 all-to-all-start.2
  449.7 41.6 %all-to-all-done.2 = f16[8,96,1120]{2,1,0:T(8,128)(2,1)S(1)} async-done(((f16[8,96,1120]{2,1,0:T(8,128)(2,1)}), f16[8,96,1120]{2,1,0:T(8,128)(2,1)S(1)}, u32[]{:S(2)}, u32[]{:S(2)}) %all-to-all-start.2) | async-done | bytes 1720352 | tf_op jit(solution)/shard_map/all_to_all | solution.py:129
  491.4 0.2 multiply_bitcast_fusion
  491.6 2.1 copy.12
  493.7 2.7 mul.27
  (2 shorter events, 0.0 us)
Async XLA Ops:
  13.1 7.4 %copy-start = (bf16[8960,96]{0,1:T(8,128)(2,1)S(1)}, bf16[8960,96]{0,1:T(8,128)(2,1)}, u32[]{:S(2)}) copy-start(bf16[8960,96]{0,1:T(8,128)(2,1)} %param.3) | copy-start | bytes 5160964
  13.1 109.1 %all-to-all-start = ((bf16[256,8,1120]{0,2,1:T(8,128)(2,1)}), bf16[256,8,1120]{0,2,1:T(8,128)(2,1)}, u32[]{:S(2)}, u32[]{:S(2)}) async-start(bf16[256,8,1120]{0,2,1:T(8,128)(2,1)} %bitcast.20), calls=%async_computation | async-start | bytes 9175040 | tf_op jit(solution)/shard_map/all_to_all | solution.py:111
  122.3 45.0 %all-to-all-start.1 = ((bf16[8,1120,96]{1,2,0:T(8,128)(2,1)}), bf16[8,1120,96]{1,2,0:T(8,128)(2,1)S(1)}, u32[]{:S(2)}, u32[]{:S(2)}) async-start(bf16[8,1120,96]{1,2,0:T(8,128)(2,1)} %copy.10), calls=%async_computation.1 | async-start | bytes 3538944 | tf_op jit(solution)/shard_map/all_to_all | solution.py:112
  125.9 163.5 %reduce-scatter.2.cloned.1.call-start = ((), (), s32[]{:S(2)}) async-start(), calls=%async_computation.4 | async-start | bytes 6488064 | tf_op jit(solution)/shard_map/reduce_scatter | solution.py:116
  175.8 185.5 %all-gather.2.cloned.1.call-start = ((), (), s32[]{:S(2)}) async-start(), calls=%async_computation.5 | async-start | bytes 6488064 | tf_op jit(solution)/shard_map/all_gather | solution.py:117
  361.4 61.6 %slice-start = ((s8[4718592]{0:T(1024)(128)(4,1)}), s8[4194304]{0:T(1024)(128)(4,1)S(1)}, s32[]{:S(2)}) async-start(s8[4718592]{0:T(1024)(128)(4,1)} %bitcast.22), calls=%async_computation.6 | async-start | bytes 8388608
  361.4 61.6 %slice-start.2 = ((s8[6291456]{0:T(1024)(128)(4,1)}), s8[4194304]{0:T(1024)(128)(4,1)S(1)}, s32[]{:S(2)}) async-start(s8[6291456]{0:T(1024)(128)(4,1)} %bitcast.28), calls=%async_computation.8 | async-start | bytes 8388608
  381.6 41.3 %slice-start.1 = ((s8[4718592]{0:T(1024)(128)(4,1)}), s8[524288]{0:T(1024)(128)(4,1)S(1)}, s32[]{:S(2)}) async-start(s8[4718592]{0:T(1024)(128)(4,1)} %bitcast.22), calls=%async_computation.7 | async-start | bytes 1048576
  381.7 41.3 %slice-start.3 = ((s8[6291456]{0:T(1024)(128)(4,1)}), s8[2097152]{0:T(1024)(128)(4,1)S(1)}, s32[]{:S(2)}) async-start(s8[6291456]{0:T(1024)(128)(4,1)} %bitcast.28), calls=%async_computation.9 | async-start | bytes 4194304
  445.7 45.7 %all-to-all-start.2 = ((f16[8,96,1120]{2,1,0:T(8,128)(2,1)}), f16[8,96,1120]{2,1,0:T(8,128)(2,1)S(1)}, u32[]{:S(2)}, u32[]{:S(2)}) async-start(f16[8,96,1120]{2,1,0:T(8,128)(2,1)} %bitcast.5), calls=%async_computation.3 | async-start | bytes 3538944 | tf_op jit(solution)/shard_map/all_to_all | solution.py:129
Sparse Core Ops, SparseCore 0:
  175.9 113.3 reduce-scatter.1
  292.6 68.6 all-gather.1

commit v3 on v2

--- a/solution.py
+++ b/solution.py
@@ -106,15 +106,46 @@
     )(gram)
 
 
+def rolled(x, start):
+    return lax.dynamic_slice_in_dim(jnp.concatenate([x, x], axis=0), start, x.shape[0], axis=0)
+
+
+def sketch_rows(slab, test_matrix):
+    z, y = lax.axis_index("z"), lax.axis_index("y")
+    n_z, n_y, n_aux = lax.axis_size("z"), lax.axis_size("y"), lax.axis_size("aux")
+    rows, width = slab.shape[0], test_matrix.shape[1]
+
+    up = [test_matrix.T]
+    down = [up[0]]
+    for s in range(1, n_z):
+        up.append(lax.ppermute(up[-1], "z", [(i, i + 1) for i in range(s - 1, n_z - 1)]))
+        down.append(lax.ppermute(down[-1], "z", [(i + 1, i) for i in range(n_z - s)]))
+    blocks = [slab]
+    for k in range(1, n_y):
+        blocks.append(lax.ppermute(slab, "y", [((i + k) % n_y, i) for i in range(n_y)]))
+
+    shards = [up[0]] + [up[s] + down[n_z - s] for s in range(1, n_z)]
+    parts = [
+        [
+            lax.dot_general(block, shard, (((1,), (1,)), ((), ())), preferred_element_type=jnp.float32)
+            for shard in shards[::-1]
+        ]
+        for block in blocks
+    ]
+    sent = jnp.stack([jnp.concatenate(p, axis=1) for p in parts])
+    sent = rolled(sent, lax.rem(n_y - y, n_y)).reshape(n_y * n_aux, rows // n_aux, n_z * width)
+    got = lax.all_to_all(sent, ("y", "aux"), split_axis=0, concat_axis=0, tiled=True)
+    summed = got.reshape(n_y, n_aux, rows // n_aux, n_z, width).sum(axis=1)
+    summed = rolled(jnp.transpose(summed, (2, 1, 0, 3)), n_z - 1 - z)
+    return jnp.transpose(summed, (1, 0, 2, 3)).reshape(rows // n_aux, n_z * n_y * width)
+
+
 def body(slab, test_matrix):
-    n_pairs = lax.axis_size("pairs")
-    slab_cols = lax.all_to_all(slab, "pairs", split_axis=1, concat_axis=0, tiled=True)
-    test_rows = lax.all_to_all(test_matrix, "pairs", split_axis=0, concat_axis=1, tiled=True)
-    largest = lax.pmax(jnp.max(jnp.abs(slab)).astype(jnp.float32), ("pairs", "aux"))
-
-    partial_value = jnp.dot(slab_cols, test_rows, preferred_element_type=jnp.float32)
-    rows = lax.psum_scatter(partial_value, ("pairs", "aux"), scatter_dimension=0, tiled=True)
-    sketch = lax.all_gather(rows, ("pairs", "aux"), axis=0, tiled=True)
+    largest = lax.pmax(jnp.max(jnp.abs(slab)).astype(jnp.float32), ("z", "y", "aux"))
+    rows = sketch_rows(slab, test_matrix)
+    slab, rows, largest = lax.optimization_barrier((slab, rows, largest))
+    slab_cols = lax.all_to_all(slab, ("z", "y"), split_axis=1, concat_axis=0, tiled=True)
+    sketch = lax.all_gather(rows, ("z", "y", "aux"), axis=0, tiled=True)
 
     gram = lax.dot_general(sketch, sketch, (((0,), (0,)), ((), ())), precision=HIGHEST, preferred_element_type=jnp.float32)
     hi, mid, lo = split3(sketch)
@@ -126,11 +157,14 @@
     bound = jnp.maximum(largest, 1e-30) * (all_rows ** 0.5)
     scale = 16384.0 / bound
     sent = (projected * scale).astype(jnp.float16)
-    got = lax.all_to_all(sent, "pairs", split_axis=0, concat_axis=1, tiled=True)
+    got = lax.all_to_all(sent, ("z", "y"), split_axis=0, concat_axis=1, tiled=True)
     return got.astype(jnp.float32) * (bound / 16384.0)
 
 
 def solution(mesh):
-    in_specs = (P("pairs", "aux"), P("aux", "pairs"))
-    out_specs = P("pairs", "aux")
-    return jax.shard_map(body, mesh=mesh, in_specs=in_specs, out_specs=out_specs, check_vma=False)
+    n_pairs, n_aux = mesh.shape["pairs"], mesh.shape["aux"]
+    n_y = 2 ** ((n_pairs.bit_length() - 1) // 2)
+    grid = jax.sharding.Mesh(mesh.devices.reshape(n_pairs // n_y, n_y, n_aux), ("z", "y", "aux"))
+    in_specs = (P(("z", "y"), "aux"), P("aux", ("z", "y")))
+    out_specs = P(("z", "y"), "aux")
+    return jax.shard_map(body, mesh=grid, in_specs=in_specs, out_specs=out_specs, check_vma=False)

time: 508 us -> 494 us (0.972)
  waiting for transfers between devices: 314 us -> 262 us
  matrix products: 48.9 us -> 67.4 us
  starting transfers between devices: 15.1 us -> 27.1 us
  Pallas kernels: 41.3 us -> 49.8 us
    reduce_scatter x1 -> x0, waiting for transfers between devices: 114 us -> none  [body(): lax.psum_scatter(partial_value, ('pairs', 'aux'), scatter_dimension=0, ti...]
    ppermute x0 -> x7, waiting for transfers between devices: none -> 92.7 us  [the longest x3 84.8 us: sketch_rows(): lax.ppermute(down[-1], 'z', [(i + 1, i) for i in range(n_z - s)])]
    all_gather x1, waiting for transfers between devices: 27.3 us -> 0.01 us  [body(): sketch = lax.all_gather(rows, ('z', 'y', 'aux'), axis=0, tiled=True)]
    dot_general x1 -> x8, matrix products: 8.49 us -> 27.2 us  [sketch_rows(): lax.dot_general(block, shard, (((1,), (1,)), ((), ())), preferred_element...]
    ppermute x0 -> x7, starting transfers between devices: none -> 14.3 us  [the longest x3 7.45 us: sketch_rows(): lax.ppermute(up[-1], 'z', [(i, i + 1) for i in range(s - 1, n_z - 1)])]
    pallas_call x1, Pallas kernels: 41.3 us -> 49.8 us  [inverse_factor(): pl.pallas_call(inverse_factor_kernel, out_shape=jax.ShapeDtypeStruct((siz...]
    optimization_barrier x0 -> x1, local copies, waits for them, and re-layouts: none -> 6.63 us  [body(): slab, rows, largest = lax.optimization_barrier((slab, rows, largest))]
    unnamed x11 -> x12, local copies, waits for them, and re-layouts: 6.62 us -> 0.03 us
  transfers between devices with their start and end apart: 5 -> 11, of which waited for: 5 -> 6; matrix products, arithmetic and copies ran while one was open for 2% -> 8% of each run, Pallas kernels for 0% -> 0%
where the time goes in v3:
time: 494 us; the launch traced here: 490 us
  waiting for transfers between devices  262 us (53%)
  matrix products  67.4 us (14%)
  Pallas kernels  49.8 us (10%)
  blocking collectives  40.5 us (8%)
  starting transfers between devices  27.1 us (5%)
  local copies, waits for them, and re-layouts  23.6 us (5%)
  between operations  14.6 us (3%)
    all_to_all x1, waiting for transfers between devices, body(): lax.all_to_all(slab, ('z', 'y'), split_axis=1, concat_axis=0, tiled=True)  128 us
    ppermute x3, waiting for transfers between devices, sketch_rows(): lax.ppermute(down[-1], 'z', [(i + 1, i) for i in range(n_z - s)])  84.8 us
    pallas_call x1, Pallas kernels, inverse_factor(): pl.pallas_call(inverse_factor_kernel, out_shape=jax.ShapeDtypeStruct((siz...  49.8 us
    all_to_all x1, waiting for transfers between devices, body(): lax.all_to_all(sent, ('z', 'y'), split_axis=0, concat_axis=1, tiled=True)  41 us
    pmax x1, blocking collectives, body(): lax.pmax(jnp.max(jnp.abs(slab)).astype(jnp.float32), ('z', 'y', 'aux'))  40.5 us
    dot_general x8, matrix products, sketch_rows(): lax.dot_general(block, shard, (((1,), (1,)), ((), ())), preferred_element...  27.2 us
    dot_general x1, matrix products, body(): lax.dot_general(sketch, sketch, (((0,), (0,)), ((), ())), precision=HIGHE...  20.2 us
    dot_general x3, matrix products, dot_t(): lax.dot_general(a, b, (((0,), (0,)), ((), ())), preferred_element_type=jn...  11.4 us
  transfers between devices with their start and end apart: 11, of which 6 were waited for; matrix products, arithmetic and copies ran while one was open for 8% of the time, Pallas kernels for 0%

profile of v3, /device:TPU:0, one launch (start us, length us, event | category | flops | bytes accessed | tf_op | source)
XLA Modules:
  0.0 489.6 jit_solution(2406246598755726968)
XLA Ops:
  6.5 3.0 collective-permute-start.6
  9.5 1.3 collective-permute-start.3
  10.8 4.7 collective-permute-start
  15.5 35.2 %collective-permute-done.3 = bf16[96,8960]{1,0:T(8,128)(2,1)S(1)} collective-permute-done((bf16[96,8960]{1,0:T(8,128)(2,1)}, bf16[96,8960]{1,0:T(8,128)(2,1)S(1)}, u32[]{:S(2)}, u32[]{:S(2)}) %collective-permute-start.3) | collective-permute-done | bytes 1720352 | tf_op jit(solution)/shard_map/ppermute | solution.py:122
  50.6 1.3 collective-permute-start.4
  51.9 1.9 collective-permute-start.1
  53.8 37.0 %collective-permute-done.4 = bf16[96,8960]{1,0:T(8,128)(2,1)} collective-permute-done((bf16[96,8960]{1,0:T(8,128)(2,1)S(1)}, bf16[96,8960]{1,0:T(8,128)(2,1)}, u32[]{:S(2)}, u32[]{:S(2)}) %collective-permute-start.4) | collective-permute-done | bytes 1720352 | tf_op jit(solution)/shard_map/ppermute | solution.py:122
  90.8 1.3 collective-permute-start.5
  92.1 4.4 fusion.15
  96.5 0.0 copy-start.1
  96.5 0.9 collective-permute-start.2
  97.4 3.5 convolution_bitcast_fusion.4
  100.9 7.9 %collective-permute-done.6 = bf16[256,8960]{1,0:T(8,128)(2,1)} collective-permute-done((bf16[256,8960]{1,0:T(8,128)(2,1)}, bf16[256,8960]{1,0:T(8,128)(2,1)}, u32[]{:S(2)}, u32[]{:S(2)}) %collective-permute-start.6) | collective-permute-done | bytes 4587552 | tf_op jit(solution)/shard_map/ppermute | solution.py:125
  108.8 3.8 fusion.16
  112.6 4.9 convolution_bitcast_fusion.1
  117.5 12.7 %collective-permute-done.5 = bf16[96,8960]{1,0:T(8,128)(2,1)S(1)} collective-permute-done((bf16[96,8960]{1,0:T(8,128)(2,1)}, bf16[96,8960]{1,0:T(8,128)(2,1)S(1)}, u32[]{:S(2)}, u32[]{:S(2)}) %collective-permute-start.5) | collective-permute-done | bytes 1720352 | tf_op jit(solution)/shard_map/ppermute | solution.py:122
  130.2 3.8 convolution_bitcast_fusion
  134.0 3.8 convolution_bitcast_fusion.2
  137.9 1.5 convolution_bitcast_fusion.3
  139.4 1.5 convolution_bitcast_fusion.5
  141.0 0.2 fusion.6
  141.2 1.1 copy.13
  142.3 3.5 all-to-all-start
  145.9 0.0 all-gather.2.cloned.1.call-start
  145.9 3.5 abs_reduce_fusion
  149.4 40.5 %pmax.7 = f32[]{:T(128)} all-reduce(bf16[]{:T(256)} %abs_reduce_fusion), channel_id=1, replica_groups=mesh['z'=4,'y'=2,'aux'=4] {'z','y','aux'}, use_global_device_ids=true, to_apply=%region_2.0 | all-reduce | flops 1 | bytes 6 | tf_op jit(solution)/shard_map/pmax | solution.py:144
  189.9 0.6 reshape.19
  190.5 0.4 reduce_sum.9
  190.9 0.3 fusion.14
  191.1 0.2 copy.14
  191.4 1.0 reshape.20
  192.4 0.0 all-gather.2.cloned.1.call-update
  192.4 6.6 %copy.15 = bf16[256,8960]{0,1:T(8,128)(2,1)} copy(bf16[256,8960]{1,0:T(8,128)(2,1)} %param.2) | data formatting | bytes 9175040 | tf_op jit(solution)/shard_map/optimization_barrier | solution.py:146
  199.0 5.6 %all-to-all-start.1 = ((bf16[256,8,1120]{0,2,1:T(8,128)(2,1)}), bf16[256,8,1120]{0,2,1:T(8,128)(2,1)}, u32[]{:S(2)}, u32[]{:S(2)}) async-start(bf16[256,8,1120]{0,2,1:T(8,128)(2,1)} %bitcast.44), calls=%async_computation.1 | async-start | bytes 9175040 | tf_op jit(solution)/shard_map/all_to_all | solution.py:147
  205.2 128.3 %all-to-all-done.1 = bf16[256,8,1120]{0,2,1:T(8,128)(2,1)} async-done(((bf16[256,8,1120]{0,2,1:T(8,128)(2,1)}), bf16[256,8,1120]{0,2,1:T(8,128)(2,1)}, u32[]{:S(2)}, u32[]{:S(2)}) %all-to-all-start.1) | async-done | bytes 4587552 | tf_op jit(solution)/shard_map/all_to_all | solution.py:147
  333.6 6.7 %copy.16 = bf16[8,256,1120]{2,1,0:T(8,128)(2,1)} copy(bf16[8,256,1120]{1,2,0:T(8,128)(2,1)} %bitcast.13) | data formatting | bytes 9175040 | tf_op jit(solution)/shard_map/all_to_all | solution.py:147
  340.3 20.2 %fusion.17.gram_ref = f32[768,768]{1,0:T(8,128)S(1)} fusion(f32[2048,768]{1,0:T(8,128)} %all-gather.2.cloned.1.call-done), kind=kOutput, calls=%fused_computation.39 | convolution fusion | flops 14495514624 | bytes 8650752 | tf_op jit(solution)/shard_map/dot_general | solution.py:150
  360.5 49.8 %shard_map.28 = f32[768,768]{1,0:T(8,128)S(1)} custom-call(f32[768,768]{1,0:T(8,128)S(1)} %fusion.17.gram_ref), custom_call_target="tpu_custom_call" | custom-call | flops 27179089920 | bytes 4718592 | tf_op jit(solution)/shard_map/pallas_call | solution.py:98
  410.4 3.8 fusion.2
  414.2 3.8 convolution_add_fusion.1
  418.0 3.8 convolution_add_fusion
  421.8 8.6 %fusion.1 = f16[768,1120]{0,1:T(8,128)(2,1)S(1)} fusion(f32[768,768]{1,0:T(8,128)S(1)} %shard_map.28, f32[768,1120]{0,1:T(8,128)S(1)} %convolution_add_fusion, f32[]{:T(128)S(6)} %div.6), kind=kOutput, calls=%fused_computation.10 | convolution fusion | flops 7928954880 | bytes 7520260 | tf_op jit(solution)/shard_map/dot_general | solution.py:154
  430.4 2.5 copy.17
  432.9 3.6 all-to-all-start.2
  436.5 41.0 %all-to-all-done.2 = f16[8,96,1120]{2,1,0:T(8,128)(2,1)S(1)} async-done(((f16[8,96,1120]{2,1,0:T(8,128)(2,1)}), f16[8,96,1120]{2,1,0:T(8,128)(2,1)S(1)}, u32[]{:S(2)}, u32[]{:S(2)}) %all-to-all-start.2) | async-done | bytes 1720352 | tf_op jit(solution)/shard_map/all_to_all | solution.py:160
  477.5 0.2 multiply_bitcast_fusion
  477.7 2.1 copy.18
  479.8 2.7 mul.27
  (20 shorter events, 0.1 us)
Async XLA Ops:
  6.5 102.3 %collective-permute-start.6 = (bf16[256,8960]{1,0:T(8,128)(2,1)}, bf16[256,8960]{1,0:T(8,128)(2,1)}, u32[]{:S(2)}, u32[]{:S(2)}) collective-permute-start(bf16[256,8960]{1,0:T(8,128)(2,1)} %param.2), channel_id=1, source_target_pairs={{4,0},{0,4},{5,1},{1,5},{6,2},{2,6},{7,3},{3,7},{12,8},{8,12},{13,... | collective-permute-start | bytes 13762568 | tf_op jit(solution)/shard_map/ppermute | solution.py:125
  9.5 41.1 %collective-permute-start.3 = (bf16[96,8960]{1,0:T(8,128)(2,1)}, bf16[96,8960]{1,0:T(8,128)(2,1)S(1)}, u32[]{:S(2)}, u32[]{:S(2)}) collective-permute-start(bf16[96,8960]{1,0:T(8,128)(2,1)} %bitcast.45), channel_id=1, source_target_pairs={{8,0},{16,8},{24,16},{9,1},{17,9},{25,17},{10,2},{18,10},{26,18},{... | collective-permute-start | bytes 5160968 | tf_op jit(solution)/shard_map/ppermute | solution.py:122
  10.8 41.1 %collective-permute-start = (bf16[96,8960]{1,0:T(8,128)(2,1)}, bf16[96,8960]{1,0:T(8,128)(2,1)S(1)}, u32[]{:S(2)}, u32[]{:S(2)}) collective-permute-start(bf16[96,8960]{1,0:T(8,128)(2,1)} %bitcast.46), channel_id=1, source_target_pairs={{0,8},{8,16},{16,24},{1,9},{9,17},{17,25},{2,10},{10,18},{18,26},{... | collective-permute-start | bytes 5160968 | tf_op jit(solution)/shard_map/ppermute | solution.py:121
  50.6 40.2 %collective-permute-start.4 = (bf16[96,8960]{1,0:T(8,128)(2,1)S(1)}, bf16[96,8960]{1,0:T(8,128)(2,1)}, u32[]{:S(2)}, u32[]{:S(2)}) collective-permute-start(bf16[96,8960]{1,0:T(8,128)(2,1)S(1)} %collective-permute-done.3), channel_id=1, source_target_pairs={{8,0},{16,8},{9,1},{17,9},{10,2},{18,10},{11,3},{19,11},{12,4},{20... | collective-permute-start | bytes 5160968 | tf_op jit(solution)/shard_map/ppermute | solution.py:122
  51.9 44.6 %collective-permute-start.1 = (bf16[96,8960]{1,0:T(8,128)(2,1)S(1)}, bf16[96,8960]{1,0:T(8,128)(2,1)}, u32[]{:S(2)}, u32[]{:S(2)}) collective-permute-start(bf16[96,8960]{1,0:T(8,128)(2,1)S(1)} %collective-permute-done), channel_id=1, source_target_pairs={{8,16},{16,24},{9,17},{17,25},{10,18},{18,26},{11,19},{19,27},{12,... | collective-permute-start | bytes 5160968 | tf_op jit(solution)/shard_map/ppermute | solution.py:121
  53.8 43.6 %copy-start = (bf16[256,8960]{1,0:T(8,128)(2,1)S(1)}, bf16[256,8960]{1,0:T(8,128)(2,1)}, u32[]{:S(2)}) copy-start(bf16[256,8960]{1,0:T(8,128)(2,1)} %param.2) | copy-start | bytes 13762564
  90.8 39.4 %collective-permute-start.5 = (bf16[96,8960]{1,0:T(8,128)(2,1)}, bf16[96,8960]{1,0:T(8,128)(2,1)S(1)}, u32[]{:S(2)}, u32[]{:S(2)}) collective-permute-start(bf16[96,8960]{1,0:T(8,128)(2,1)} %collective-permute-done.4), channel_id=1, source_target_pairs={{8,0},{9,1},{10,2},{11,3},{12,4},{13,5},{14,6},{15,7}} | collective-permute-start | bytes 5160968 | tf_op jit(solution)/shard_map/ppermute | solution.py:122
  96.5 12.3 %copy-start.1 = (bf16[8960,96]{0,1:T(8,128)(2,1)S(1)}, bf16[8960,96]{0,1:T(8,128)(2,1)}, u32[]{:S(2)}) copy-start(bf16[8960,96]{0,1:T(8,128)(2,1)} %param.3) | copy-start | bytes 5160964
  96.5 37.5 %collective-permute-start.2 = (bf16[96,8960]{1,0:T(8,128)(2,1)}, bf16[96,8960]{1,0:T(8,128)(2,1)S(1)}, u32[]{:S(2)}, u32[]{:S(2)}) collective-permute-start(bf16[96,8960]{1,0:T(8,128)(2,1)} %collective-permute-done.1), channel_id=1, source_target_pairs={{16,24},{17,25},{18,26},{19,27},{20,28},{21,29},{22,30},{23,31}} | collective-permute-start | bytes 5160968 | tf_op jit(solution)/shard_map/ppermute | solution.py:121
  142.3 47.6 %all-to-all-start = ((f32[8,64,384]{2,1,0:T(8,128)}), f32[8,64,384]{2,1,0:T(8,128)S(1)}, u32[]{:S(2)}, u32[]{:S(2)}) async-start(f32[8,64,384]{2,1,0:T(8,128)} %bitcast.9), calls=%async_computation | async-start | bytes 1572864 | tf_op jit(solution)/shard_map/all_to_all | solution.py:137
  145.9 194.4 %all-gather.2.cloned.1.call-start = ((), (), s32[]{:S(2)}) async-start(), calls=%async_computation.3 | async-start | bytes 6488064 | tf_op jit(solution)/shard_map/all_gather | solution.py:148
  199.0 134.6 %all-to-all-start.1 = ((bf16[256,8,1120]{0,2,1:T(8,128)(2,1)}), bf16[256,8,1120]{0,2,1:T(8,128)(2,1)}, u32[]{:S(2)}, u32[]{:S(2)}) async-start(bf16[256,8,1120]{0,2,1:T(8,128)(2,1)} %bitcast.44), calls=%async_computation.1 | async-start | bytes 9175040 | tf_op jit(solution)/shard_map/all_to_all | solution.py:147
  340.3 70.1 %slice-start = ((s8[4718592]{0:T(1024)(128)(4,1)}), s8[4194304]{0:T(1024)(128)(4,1)S(1)}, s32[]{:S(2)}) async-start(s8[4718592]{0:T(1024)(128)(4,1)} %bitcast.47), calls=%async_computation.4 | async-start | bytes 8388608
  340.3 70.1 %slice-start.2 = ((s8[6291456]{0:T(1024)(128)(4,1)}), s8[4194304]{0:T(1024)(128)(4,1)S(1)}, s32[]{:S(2)}) async-start(s8[6291456]{0:T(1024)(128)(4,1)} %bitcast.53), calls=%async_computation.6 | async-start | bytes 8388608
  360.5 49.9 %slice-start.1 = ((s8[4718592]{0:T(1024)(128)(4,1)}), s8[524288]{0:T(1024)(128)(4,1)S(1)}, s32[]{:S(2)}) async-start(s8[4718592]{0:T(1024)(128)(4,1)} %bitcast.47), calls=%async_computation.5 | async-start | bytes 1048576
  360.5 49.9 %slice-start.3 = ((s8[6291456]{0:T(1024)(128)(4,1)}), s8[2097152]{0:T(1024)(128)(4,1)S(1)}, s32[]{:S(2)}) async-start(s8[6291456]{0:T(1024)(128)(4,1)} %bitcast.53), calls=%async_computation.7 | async-start | bytes 4194304
  432.9 44.6 %all-to-all-start.2 = ((f16[8,96,1120]{2,1,0:T(8,128)(2,1)}), f16[8,96,1120]{2,1,0:T(8,128)(2,1)S(1)}, u32[]{:S(2)}, u32[]{:S(2)}) async-start(f16[8,96,1120]{2,1,0:T(8,128)(2,1)} %bitcast.15), calls=%async_computation.2 | async-start | bytes 3538944 | tf_op jit(solution)/shard_map/all_to_all | solution.py:160
Sparse Core Ops, SparseCore 0:
  192.5 144.9 all-gather.1

commit v4 on v3

--- a/solution.py
+++ b/solution.py
@@ -110,6 +110,11 @@
     return lax.dynamic_slice_in_dim(jnp.concatenate([x, x], axis=0), start, x.shape[0], axis=0)
 
 
+def gathered_max(slab):
+    own = jnp.full((8, 128), jnp.max(jnp.abs(slab)).astype(jnp.float32))
+    return jnp.max(lax.all_gather(own, ("z", "y")))
+
+
 def sketch_rows(slab, test_matrix):
     z, y = lax.axis_index("z"), lax.axis_index("y")
     n_z, n_y, n_aux = lax.axis_size("z"), lax.axis_size("y"), lax.axis_size("aux")
@@ -124,6 +129,9 @@
     for k in range(1, n_y):
         blocks.append(lax.ppermute(slab, "y", [((i + k) % n_y, i) for i in range(n_y)]))
 
+    up[-1], down[-1], later, largest = lax.optimization_barrier((up[-1], down[-1], slab, gathered_max(slab)))
+    slab_cols = lax.all_to_all(later, ("z", "y"), split_axis=1, concat_axis=0, tiled=True)
+
     shards = [up[0]] + [up[s] + down[n_z - s] for s in range(1, n_z)]
     parts = [
         [
@@ -133,18 +141,28 @@
         for block in blocks
     ]
     sent = jnp.stack([jnp.concatenate(p, axis=1) for p in parts])
-    sent = rolled(sent, lax.rem(n_y - y, n_y)).reshape(n_y * n_aux, rows // n_aux, n_z * width)
-    got = lax.all_to_all(sent, ("y", "aux"), split_axis=0, concat_axis=0, tiled=True)
-    summed = got.reshape(n_y, n_aux, rows // n_aux, n_z, width).sum(axis=1)
-    summed = rolled(jnp.transpose(summed, (2, 1, 0, 3)), n_z - 1 - z)
-    return jnp.transpose(summed, (1, 0, 2, 3)).reshape(rows // n_aux, n_z * n_y * width)
+    sent = rolled(sent, lax.rem(n_y - y, n_y)).reshape(n_y, n_aux, rows // n_aux, n_z * width)
+
+    aux = lax.axis_index("aux")
+
+    def exchange(dy, da):
+        piece = lax.dynamic_slice(sent, (y ^ dy, aux ^ da, 0, 0), (1, 1) + sent.shape[2:])[0, 0]
+        if dy or da:
+            pairs = [(i * n_aux + j, (i ^ dy) * n_aux + (j ^ da)) for i in range(n_y) for j in range(n_aux)]
+            piece = lax.ppermute(piece, ("y", "aux"), pairs)
+        return piece
+
+    own_y = [sum(exchange(dy, da) for da in range(n_aux)) for dy in range(n_y)]
+    summed = jnp.stack(own_y)
+    summed = jnp.stack([lax.dynamic_index_in_dim(summed, y ^ k, keepdims=False) for k in range(n_y)])
+    summed = jnp.transpose(summed.reshape(n_y, rows // n_aux, n_z, width), (2, 1, 0, 3))
+    summed = rolled(summed, n_z - 1 - z)
+    summed = jnp.transpose(summed, (1, 0, 2, 3)).reshape(rows // n_aux, n_z * n_y * width)
+    return summed, slab_cols, largest
 
 
 def body(slab, test_matrix):
-    largest = lax.pmax(jnp.max(jnp.abs(slab)).astype(jnp.float32), ("z", "y", "aux"))
-    rows = sketch_rows(slab, test_matrix)
-    slab, rows, largest = lax.optimization_barrier((slab, rows, largest))
-    slab_cols = lax.all_to_all(slab, ("z", "y"), split_axis=1, concat_axis=0, tiled=True)
+    rows, slab_cols, largest = sketch_rows(slab, test_matrix)
     sketch = lax.all_gather(rows, ("z", "y", "aux"), axis=0, tiled=True)
 
     gram = lax.dot_general(sketch, sketch, (((0,), (0,)), ((), ())), precision=HIGHEST, preferred_element_type=jnp.float32)

time: 494 us -> 488 us (0.988)
  waiting for transfers between devices: 262 us -> 235 us
  blocking collectives: 40.5 us -> 61.8 us
  Pallas kernels: 49.8 us -> 41.3 us
    ppermute x3, waiting for transfers between devices: 84.8 us -> 22.9 us  [sketch_rows(): lax.ppermute(down[-1], 'z', [(i + 1, i) for i in range(n_z - s)])]
    unnamed x0 -> x1, blocking collectives: none -> 61.8 us
    pmax x1 -> x0, blocking collectives: 40.5 us -> none  [body(): lax.pmax(jnp.max(jnp.abs(slab)).astype(jnp.float32), ('z', 'y', 'aux'))]
    ppermute x3, waiting for transfers between devices: 0.01 us -> 35.4 us  [sketch_rows(): lax.ppermute(up[-1], 'z', [(i, i + 1) for i in range(s - 1, n_z - 1)])]
    pallas_call x1, Pallas kernels: 49.8 us -> 41.3 us  [inverse_factor(): pl.pallas_call(inverse_factor_kernel, out_shape=jax.ShapeDtypeStruct((siz...]
    ppermute x1, waiting for transfers between devices: 7.88 us -> 0.01 us  [sketch_rows(): lax.ppermute(slab, 'y', [((i + k) % n_y, i) for i in range(n_y)])]
    ppermute x0 -> x7, waiting for transfers between devices: none -> 7.17 us  [exchange(): piece = lax.ppermute(piece, ('y', 'aux'), pairs)]
    ppermute x0 -> x7, starting transfers between devices: none -> 5.52 us  [exchange(): piece = lax.ppermute(piece, ('y', 'aux'), pairs)]
  transfers between devices with their start and end apart: 11 -> 17, of which waited for: 6 -> 9; matrix products, arithmetic and copies ran while one was open for 8% -> 8% of each run, Pallas kernels for 0% -> 0%
where the time goes in v4:
time: 488 us; the launch traced here: 479 us
  waiting for transfers between devices  235 us (48%)
  matrix products  68.9 us (14%)
  blocking collectives  61.8 us (13%)
  Pallas kernels  41.3 us (8%)
  starting transfers between devices  27.1 us (6%)
  local copies, waits for them, and re-layouts  23.5 us (5%)
  between operations  15 us (3%)
  other arithmetic  6.45 us (1%)
    all_to_all x1, waiting for transfers between devices, sketch_rows(): lax.all_to_all(later, ('z', 'y'), split_axis=1, concat_axis=0, tiled=True)  129 us
    unnamed x1, blocking collectives  61.8 us
    all_to_all x1, waiting for transfers between devices, body(): lax.all_to_all(sent, ('z', 'y'), split_axis=0, concat_axis=1, tiled=True)  41.4 us
    pallas_call x1, Pallas kernels, inverse_factor(): pl.pallas_call(inverse_factor_kernel, out_shape=jax.ShapeDtypeStruct((siz...  41.3 us
    ppermute x3, waiting for transfers between devices, sketch_rows(): lax.ppermute(up[-1], 'z', [(i, i + 1) for i in range(s - 1, n_z - 1)])  35.4 us
    dot_general x8, matrix products, sketch_rows(): lax.dot_general(block, shard, (((1,), (1,)), ((), ())), preferred_element...  28.7 us
    ppermute x3, waiting for transfers between devices, sketch_rows(): lax.ppermute(down[-1], 'z', [(i + 1, i) for i in range(n_z - s)])  22.9 us
    dot_general x1, matrix products, body(): lax.dot_general(sketch, sketch, (((0,), (0,)), ((), ())), precision=HIGHE...  20.2 us
  transfers between devices with their start and end apart: 17, of which 9 were waited for; matrix products, arithmetic and copies ran while one was open for 8% of the time, Pallas kernels for 0%

profile of v4, /device:TPU:0, one launch (start us, length us, event | category | flops | bytes accessed | tf_op | source)
XLA Modules:
  0.0 479.5 jit_solution(12808867038439488160)
XLA Ops:
  6.5 3.0 collective-permute-start.6
  9.5 3.6 collective-permute-start
  13.1 1.3 collective-permute-start.3
  14.4 35.4 %collective-permute-done = bf16[96,8960]{1,0:T(8,128)(2,1)S(1)} collective-permute-done((bf16[96,8960]{1,0:T(8,128)(2,1)}, bf16[96,8960]{1,0:T(8,128)(2,1)S(1)}, u32[]{:S(2)}, u32[]{:S(2)}) %collective-permute-start) | collective-permute-done | bytes 1720352 | tf_op jit(solution)/shard_map/ppermute | solution.py:126
  49.8 1.9 collective-permute-start.1
  51.7 2.3 collective-permute-done.3
  54.0 1.3 collective-permute-start.4
  55.3 1.2 dynamic-slice
  56.6 3.5 abs_reduce_fusion
  60.1 1.3 convert_dynamic-update-slice_fusion
  61.5 61.8 %all-reduce = f32[8]{0:T(128)S(1)} all-reduce(f32[8]{0:T(128)S(1)} %convert_dynamic-update-slice_fusion), channel_id=2, replica_groups=mesh['z'=4,'y'=2,'aux'=4] {'z','y'}, use_global_device_ids=true, to_apply=%add | all-reduce | flops 8 | bytes 64
  123.3 0.7 broadcast_reduce_fusion
  124.0 0.9 collective-permute-start.2
  124.9 1.3 collective-permute-start.5
  126.2 3.8 fusion.20
  130.1 3.5 convolution_bitcast_fusion.4
  133.6 3.8 fusion.21
  137.4 4.9 %convolution_bitcast_fusion.1 = f32[256,96]{0,1:T(8,128)S(1)} fusion(bf16[256,8960]{1,0:T(8,128)(2,1)} %collective-permute-done.6, bf16[96,8960]{1,0:T(8,128)(2,1)} %collective-permute-done.1, bf16[96,8960]{1,0:T(8,128)(2,1)} %collective-permute-done.4), kind=kOutput, calls=%fused_computation.17 | convolution fusion | flops 441262080 | bytes 8126464 | tf_op jit(solution)/shard_map/dot_general | solution.py:138
  142.3 20.6 %collective-permute-done.5 = bf16[96,8960]{1,0:T(8,128)(2,1)S(1)} collective-permute-done((bf16[96,8960]{1,0:T(8,128)(2,1)}, bf16[96,8960]{1,0:T(8,128)(2,1)S(1)}, u32[]{:S(2)}, u32[]{:S(2)}) %collective-permute-start.5) | collective-permute-done | bytes 1720352 | tf_op jit(solution)/shard_map/ppermute | solution.py:127
  162.9 4.3 convolution_bitcast_fusion.2
  167.3 3.8 convolution_bitcast_fusion
  171.1 3.0 convolution_bitcast_fusion.5
  174.1 1.5 convolution_bitcast_fusion.3
  176.3 1.6 collective-permute-start.8
  177.8 0.3 collective-permute-start.9
  178.1 1.7 collective-permute-start.11
  179.8 1.3 collective-permute-start.12
  181.1 0.8 collective-permute-done.8
  181.9 0.6 collective-permute-start.13
  182.5 0.6 collective-permute-done.9
  183.2 0.6 collective-permute-done.10
  183.8 5.2 %collective-permute-done.11 = f32[64,384]{1,0:T(8,128)S(1)} collective-permute-done((f32[64,384]{1,0:T(8,128)S(1)}, f32[64,384]{1,0:T(8,128)S(1)}, u32[]{:S(2)}, u32[]{:S(2)}) %collective-permute-start.11) | collective-permute-done | bytes 98336 | tf_op jit(solution)/shard_map/ppermute | solution.py:152
  189.7 1.0 reshape.20
  190.7 6.6 %copy.16 = bf16[256,8960]{0,1:T(8,128)(2,1)} copy(bf16[256,8960]{1,0:T(8,128)(2,1)} %param.2) | data formatting | bytes 9175040 | tf_op jit(solution)/shard_map/optimization_barrier | solution.py:132
  197.3 4.8 all-to-all-start
  202.8 128.5 %all-to-all-done = bf16[256,8,1120]{0,2,1:T(8,128)(2,1)} async-done(((bf16[256,8,1120]{0,2,1:T(8,128)(2,1)}), bf16[256,8,1120]{0,2,1:T(8,128)(2,1)}, u32[]{:S(2)}, u32[]{:S(2)}) %all-to-all-start) | async-done | bytes 4587552 | tf_op jit(solution)/shard_map/all_to_all | solution.py:133
  331.4 6.6 %copy.17 = bf16[8,256,1120]{2,1,0:T(8,128)(2,1)} copy(bf16[8,256,1120]{1,2,0:T(8,128)(2,1)} %bitcast.25) | data formatting | bytes 9175040 | tf_op jit(solution)/shard_map/all_to_all | solution.py:133
  338.0 20.2 %fusion.22.gram_ref = f32[768,768]{1,0:T(8,128)S(1)} fusion(f32[2048,768]{1,0:T(8,128)} %all-gather.2.cloned.1.call-done), kind=kOutput, calls=%fused_computation.60 | convolution fusion | flops 14495514624 | bytes 8650752 | tf_op jit(solution)/shard_map/dot_general | solution.py:168
  358.3 41.3 %shard_map.28 = f32[768,768]{1,0:T(8,128)S(1)} custom-call(f32[768,768]{1,0:T(8,128)S(1)} %fusion.22.gram_ref), custom_call_target="tpu_custom_call" | custom-call | flops 27179089920 | bytes 4718592 | tf_op jit(solution)/shard_map/pallas_call | solution.py:98
  399.6 3.8 fusion.2
  403.4 3.8 convolution_add_fusion.1
  407.2 3.8 convolution_add_fusion
  411.0 8.6 %fusion.1 = f16[768,1120]{0,1:T(8,128)(2,1)S(1)} fusion(f32[768,768]{1,0:T(8,128)S(1)} %shard_map.28, f32[768,1120]{0,1:T(8,128)S(1)} %convolution_add_fusion, f32[]{:T(128)S(6)} %div.6), kind=kOutput, calls=%fused_computation.10 | convolution fusion | flops 7928954880 | bytes 7520260 | tf_op jit(solution)/shard_map/dot_general | solution.py:172
  419.7 2.5 copy.18
  422.1 3.6 all-to-all-start.1
  425.7 41.4 %all-to-all-done.1 = f16[8,96,1120]{2,1,0:T(8,128)(2,1)S(1)} async-done(((f16[8,96,1120]{2,1,0:T(8,128)(2,1)}), f16[8,96,1120]{2,1,0:T(8,128)(2,1)S(1)}, u32[]{:S(2)}, u32[]{:S(2)}) %all-to-all-start.1) | async-done | bytes 1720352 | tf_op jit(solution)/shard_map/all_to_all | solution.py:178
  467.4 2.1 copy.19
  469.5 2.7 mul.27
  (40 shorter events, 1.7 us)
Async XLA Ops:
  6.5 119.7 %copy-start.1 = (bf16[8960,96]{0,1:T(8,128)(2,1)S(1)}, bf16[8960,96]{0,1:T(8,128)(2,1)}, u32[]{:S(2)}) copy-start(bf16[8960,96]{0,1:T(8,128)(2,1)} %param.3) | copy-start | bytes 5160964
  6.5 331.5 %all-gather.2.cloned.1.call-start = ((), (), s32[]{:S(2)}) async-start(), calls=%async_computation.2 | async-start | bytes 6488064 | tf_op jit(solution)/shard_map/all_gather | solution.py:166
  6.5 127.1 %collective-permute-start.6 = (bf16[256,8960]{1,0:T(8,128)(2,1)}, bf16[256,8960]{1,0:T(8,128)(2,1)}, u32[]{:S(2)}, u32[]{:S(2)}) collective-permute-start(bf16[256,8960]{1,0:T(8,128)(2,1)} %param.2), channel_id=1, source_target_pairs={{4,0},{0,4},{5,1},{1,5},{6,2},{2,6},{7,3},{3,7},{12,8},{8,12},{13,... | collective-permute-start | bytes 13762568 | tf_op jit(solution)/shard_map/ppermute | solution.py:130
  9.5 40.3 %collective-permute-start = (bf16[96,8960]{1,0:T(8,128)(2,1)}, bf16[96,8960]{1,0:T(8,128)(2,1)S(1)}, u32[]{:S(2)}, u32[]{:S(2)}) collective-permute-start(bf16[96,8960]{1,0:T(8,128)(2,1)} %bitcast.74), channel_id=1, source_target_pairs={{0,8},{8,16},{16,24},{1,9},{9,17},{17,25},{2,10},{10,18},{18,26},{... | collective-permute-start | bytes 5160968 | tf_op jit(solution)/shard_map/ppermute | solution.py:126
  13.1 40.9 %collective-permute-start.3 = (bf16[96,8960]{1,0:T(8,128)(2,1)}, bf16[96,8960]{1,0:T(8,128)(2,1)}, u32[]{:S(2)}, u32[]{:S(2)}) collective-permute-start(bf16[96,8960]{1,0:T(8,128)(2,1)} %bitcast.75), channel_id=1, source_target_pairs={{8,0},{16,8},{24,16},{9,1},{17,9},{25,17},{10,2},{18,10},{26,18},{... | collective-permute-start | bytes 5160968 | tf_op jit(solution)/shard_map/ppermute | solution.py:127
  49.8 74.2 %collective-permute-start.1 = (bf16[96,8960]{1,0:T(8,128)(2,1)S(1)}, bf16[96,8960]{1,0:T(8,128)(2,1)}, u32[]{:S(2)}, u32[]{:S(2)}) collective-permute-start(bf16[96,8960]{1,0:T(8,128)(2,1)S(1)} %collective-permute-done), channel_id=1, source_target_pairs={{8,16},{16,24},{9,17},{17,25},{10,18},{18,26},{11,19},{19,27},{12,... | collective-permute-start | bytes 5160968 | tf_op jit(solution)/shard_map/ppermute | solution.py:126
  54.0 70.9 %collective-permute-start.4 = (bf16[96,8960]{1,0:T(8,128)(2,1)}, bf16[96,8960]{1,0:T(8,128)(2,1)}, u32[]{:S(2)}, u32[]{:S(2)}) collective-permute-start(bf16[96,8960]{1,0:T(8,128)(2,1)} %collective-permute-done.3), channel_id=1, source_target_pairs={{8,0},{16,8},{9,1},{17,9},{10,2},{18,10},{11,3},{19,11},{12,4},{20... | collective-permute-start | bytes 5160968 | tf_op jit(solution)/shard_map/ppermute | solution.py:127
  123.3 6.8 %copy-start = (bf16[256,8960]{1,0:T(8,128)(2,1)S(1)}, bf16[256,8960]{1,0:T(8,128)(2,1)}, u32[]{:S(2)}) copy-start(bf16[256,8960]{1,0:T(8,128)(2,1)} %param.2) | copy-start | bytes 13762564
  124.0 18.3 %collective-permute-start.2 = (bf16[96,8960]{1,0:T(8,128)(2,1)}, bf16[96,8960]{1,0:T(8,128)(2,1)S(1)}, u32[]{:S(2)}, u32[]{:S(2)}) collective-permute-start(bf16[96,8960]{1,0:T(8,128)(2,1)} %collective-permute-done.1), channel_id=1, source_target_pairs={{16,24},{17,25},{18,26},{19,27},{20,28},{21,29},{22,30},{23,31}} | collective-permute-start | bytes 5160968 | tf_op jit(solution)/shard_map/ppermute | solution.py:126
  124.9 38.0 %collective-permute-start.5 = (bf16[96,8960]{1,0:T(8,128)(2,1)}, bf16[96,8960]{1,0:T(8,128)(2,1)S(1)}, u32[]{:S(2)}, u32[]{:S(2)}) collective-permute-start(bf16[96,8960]{1,0:T(8,128)(2,1)} %collective-permute-done.4), channel_id=1, source_target_pairs={{8,0},{9,1},{10,2},{11,3},{12,4},{13,5},{14,6},{15,7}} | collective-permute-start | bytes 5160968 | tf_op jit(solution)/shard_map/ppermute | solution.py:127
  176.2 3.6 collective-permute-start.7
  176.3 5.7 %collective-permute-start.8 = (f32[64,384]{1,0:T(8,128)S(1)}, f32[64,384]{1,0:T(8,128)S(1)}, u32[]{:S(2)}, u32[]{:S(2)}) collective-permute-start(f32[64,384]{1,0:T(8,128)S(1)} %get-tuple-element.18), channel_id=1, source_target_pairs={{0,2},{1,3},{2,0},{3,1},{4,6},{5,7},{6,4},{7,5},{8,10},{9,11},{10,... | collective-permute-start | bytes 294920 | tf_op jit(solution)/shard_map/ppermute | solution.py:152
  177.8 5.3 %collective-permute-start.9 = (f32[64,384]{1,0:T(8,128)S(1)}, f32[64,384]{1,0:T(8,128)S(1)}, u32[]{:S(2)}, u32[]{:S(2)}) collective-permute-start(f32[64,384]{1,0:T(8,128)S(1)} %get-tuple-element.17), channel_id=1, source_target_pairs={{0,3},{1,2},{2,1},{3,0},{4,7},{5,6},{6,5},{7,4},{8,11},{9,10},{10,... | collective-permute-start | bytes 294920 | tf_op jit(solution)/shard_map/ppermute | solution.py:152
  178.1 5.6 %collective-permute-start.10 = (f32[64,384]{1,0:T(8,128)S(1)}, f32[64,384]{1,0:T(8,128)S(1)}, u32[]{:S(2)}, u32[]{:S(2)}) collective-permute-start(f32[64,384]{1,0:T(8,128)S(1)} %get-tuple-element.16), channel_id=1, source_target_pairs={{0,4},{1,5},{2,6},{3,7},{4,0},{5,1},{6,2},{7,3},{8,12},{9,13},{10,... | collective-permute-start | bytes 294920 | tf_op jit(solution)/shard_map/ppermute | solution.py:152
  178.1 10.8 %collective-permute-start.11 = (f32[64,384]{1,0:T(8,128)S(1)}, f32[64,384]{1,0:T(8,128)S(1)}, u32[]{:S(2)}, u32[]{:S(2)}) collective-permute-start(f32[64,384]{1,0:T(8,128)S(1)} %get-tuple-element.13), channel_id=1, source_target_pairs={{0,5},{1,4},{2,7},{3,6},{4,1},{5,0},{6,3},{7,2},{8,13},{9,12},{10,... | collective-permute-start | bytes 294920 | tf_op jit(solution)/shard_map/ppermute | solution.py:152
  179.8 9.1 %collective-permute-start.12 = (f32[64,384]{1,0:T(8,128)S(1)}, f32[64,384]{1,0:T(8,128)S(1)}, u32[]{:S(2)}, u32[]{:S(2)}) collective-permute-start(f32[64,384]{1,0:T(8,128)S(1)} %get-tuple-element.15), channel_id=1, source_target_pairs={{0,6},{1,7},{2,4},{3,5},{4,2},{5,3},{6,0},{7,1},{8,14},{9,15},{10,... | collective-permute-start | bytes 294920 | tf_op jit(solution)/shard_map/ppermute | solution.py:152
  181.9 7.0 %collective-permute-start.13 = (f32[64,384]{1,0:T(8,128)S(1)}, f32[64,384]{1,0:T(8,128)S(1)}, u32[]{:S(2)}, u32[]{:S(2)}) collective-permute-start(f32[64,384]{1,0:T(8,128)S(1)} %get-tuple-element.14), channel_id=1, source_target_pairs={{0,7},{1,6},{2,5},{3,4},{4,3},{5,2},{6,1},{7,0},{8,15},{9,14},{10,... | collective-permute-start | bytes 294920 | tf_op jit(solution)/shard_map/ppermute | solution.py:152
  197.3 134.0 %all-to-all-start = ((bf16[256,8,1120]{0,2,1:T(8,128)(2,1)}), bf16[256,8,1120]{0,2,1:T(8,128)(2,1)}, u32[]{:S(2)}, u32[]{:S(2)}) async-start(bf16[256,8,1120]{0,2,1:T(8,128)(2,1)} %bitcast.73), calls=%async_computation | async-start | bytes 9175040 | tf_op jit(solution)/shard_map/all_to_all | solution.py:133
  338.0 61.5 %slice-start = ((s8[4718592]{0:T(1024)(128)(4,1)}), s8[4194304]{0:T(1024)(128)(4,1)S(1)}, s32[]{:S(2)}) async-start(s8[4718592]{0:T(1024)(128)(4,1)} %bitcast.76), calls=%async_computation.3 | async-start | bytes 8388608
  338.0 61.5 %slice-start.2 = ((s8[6291456]{0:T(1024)(128)(4,1)}), s8[4194304]{0:T(1024)(128)(4,1)S(1)}, s32[]{:S(2)}) async-start(s8[6291456]{0:T(1024)(128)(4,1)} %bitcast.84), calls=%async_computation.5 | async-start | bytes 8388608
  358.2 41.3 %slice-start.1 = ((s8[4718592]{0:T(1024)(128)(4,1)}), s8[524288]{0:T(1024)(128)(4,1)S(1)}, s32[]{:S(2)}) async-start(s8[4718592]{0:T(1024)(128)(4,1)} %bitcast.76), calls=%async_computation.4 | async-start | bytes 1048576
  358.2 41.3 %slice-start.3 = ((s8[6291456]{0:T(1024)(128)(4,1)}), s8[2097152]{0:T(1024)(128)(4,1)S(1)}, s32[]{:S(2)}) async-start(s8[6291456]{0:T(1024)(128)(4,1)} %bitcast.84), calls=%async_computation.6 | async-start | bytes 4194304
  422.1 45.0 %all-to-all-start.1 = ((f16[8,96,1120]{2,1,0:T(8,128)(2,1)}), f16[8,96,1120]{2,1,0:T(8,128)(2,1)S(1)}, u32[]{:S(2)}, u32[]{:S(2)}) async-start(f16[8,96,1120]{2,1,0:T(8,128)(2,1)} %bitcast.27), calls=%async_computation.1 | async-start | bytes 3538944 | tf_op jit(solution)/shard_map/all_to_all | solution.py:178
Sparse Core Ops, SparseCore 0:
  190.8 144.4 all-gather.1

commit v5 on v4

--- a/solution.py
+++ b/solution.py
@@ -2,6 +2,7 @@
 import jax.numpy as jnp
 from jax import lax
 from jax.experimental import pallas as pl
+from jax.experimental.layout import Layout, with_layout_constraint
 from jax.experimental.pallas import tpu as pltpu
 from jax.sharding import PartitionSpec as P
 
@@ -110,73 +111,108 @@
     return lax.dynamic_slice_in_dim(jnp.concatenate([x, x], axis=0), start, x.shape[0], axis=0)
 
 
-def gathered_max(slab):
-    own = jnp.full((8, 128), jnp.max(jnp.abs(slab)).astype(jnp.float32))
-    return jnp.max(lax.all_gather(own, ("z", "y")))
-
-
-def sketch_rows(slab, test_matrix):
-    z, y = lax.axis_index("z"), lax.axis_index("y")
+def row_major(x):
+    return with_layout_constraint(x, Layout(major_to_minor=tuple(range(x.ndim))))
+
+
+def tie(*arrays):
+    return lax.optimization_barrier(arrays)
+
+
+def body(slab, test_matrix):
+    z, y, aux = lax.axis_index("z"), lax.axis_index("y"), lax.axis_index("aux")
     n_z, n_y, n_aux = lax.axis_size("z"), lax.axis_size("y"), lax.axis_size("aux")
     rows, width = slab.shape[0], test_matrix.shape[1]
+    n_cols = slab.shape[1] // (n_z * n_y)
 
     up = [test_matrix.T]
     down = [up[0]]
+    blocks = [row_major(slab.T)]
+    for k in range(1, n_y):
+        blocks.append(lax.ppermute(blocks[0], "y", [((i + k) % n_y, i) for i in range(n_y)]))
+
+    def piece(to_z):
+        start = (to_z * n_y + y) * n_cols
+        return jnp.stack([lax.dynamic_slice(b, (start, 0), (n_cols, rows)) for b in blocks])
+
+    def send(d, firsts):
+        ups = [(i, i + d) for i in firsts]
+        downs = [(n_z - 1 - i, n_z - 1 - j) for i, j in ups]
+        return [(d, lax.ppermute(above[d], "z", ups)), (n_z - d, lax.ppermute(below[d], "z", downs))]
+
     for s in range(1, n_z):
+        if s == n_z - 1:
+            above = {d: piece(z + d) for d in range(1, n_z)}
+            below = {d: piece(z - d) for d in range(1, n_z)}
+            above[1], below[1], up[-1], down[-1] = tie(above[1], below[1], up[-1], down[-1])
+            moved = send(1, range(n_z - 2))
         up.append(lax.ppermute(up[-1], "z", [(i, i + 1) for i in range(s - 1, n_z - 1)]))
         down.append(lax.ppermute(down[-1], "z", [(i + 1, i) for i in range(n_z - s)]))
-    blocks = [slab]
-    for k in range(1, n_y):
-        blocks.append(lax.ppermute(slab, "y", [((i + k) % n_y, i) for i in range(n_y)]))
-
-    up[-1], down[-1], later, largest = lax.optimization_barrier((up[-1], down[-1], slab, gathered_max(slab)))
-    slab_cols = lax.all_to_all(later, ("z", "y"), split_axis=1, concat_axis=0, tiled=True)
+
+    above[1], below[1], above[2], below[2], up[-1], down[-1] = tie(above[1], below[1], above[2], below[2], up[-1], down[-1])
+    second = send(1, [n_z - 2]) + send(2, [0])
 
     shards = [up[0]] + [up[s] + down[n_z - s] for s in range(1, n_z)]
-    parts = [
+    sent = jnp.stack(
         [
-            lax.dot_general(block, shard, (((1,), (1,)), ((), ())), preferred_element_type=jnp.float32)
-            for shard in shards[::-1]
+            jnp.concatenate([jnp.dot(shard, block, preferred_element_type=jnp.float32) for shard in shards[::-1]], axis=0).T
+            for block in blocks
         ]
-        for block in blocks
-    ]
-    sent = jnp.stack([jnp.concatenate(p, axis=1) for p in parts])
+    )
     sent = rolled(sent, lax.rem(n_y - y, n_y)).reshape(n_y, n_aux, rows // n_aux, n_z * width)
 
-    aux = lax.axis_index("aux")
-
     def exchange(dy, da):
-        piece = lax.dynamic_slice(sent, (y ^ dy, aux ^ da, 0, 0), (1, 1) + sent.shape[2:])[0, 0]
+        part = lax.dynamic_slice(sent, (y ^ dy, aux ^ da, 0, 0), (1, 1) + sent.shape[2:])[0, 0]
         if dy or da:
             pairs = [(i * n_aux + j, (i ^ dy) * n_aux + (j ^ da)) for i in range(n_y) for j in range(n_aux)]
-            piece = lax.ppermute(piece, ("y", "aux"), pairs)
-        return piece
-
-    own_y = [sum(exchange(dy, da) for da in range(n_aux)) for dy in range(n_y)]
-    summed = jnp.stack(own_y)
+            part = lax.ppermute(part, ("y", "aux"), pairs)
+        return part
+
+    summed = jnp.stack([sum(exchange(dy, da) for da in range(n_aux)) for dy in range(n_y)])
     summed = jnp.stack([lax.dynamic_index_in_dim(summed, y ^ k, keepdims=False) for k in range(n_y)])
     summed = jnp.transpose(summed.reshape(n_y, rows // n_aux, n_z, width), (2, 1, 0, 3))
     summed = rolled(summed, n_z - 1 - z)
-    summed = jnp.transpose(summed, (1, 0, 2, 3)).reshape(rows // n_aux, n_z * n_y * width)
-    return summed, slab_cols, largest
-
-
-def body(slab, test_matrix):
-    rows, slab_cols, largest = sketch_rows(slab, test_matrix)
-    sketch = lax.all_gather(rows, ("z", "y", "aux"), axis=0, tiled=True)
+    own_rows = jnp.transpose(summed, (1, 0, 2, 3)).reshape(rows // n_aux, n_z * n_y * width)
+
+    tied = tie(own_rows, *[x for _, x in second])
+    moved += [(s, x) for (s, _), x in zip(second, tied[1:])]
+    sketch = lax.all_gather(tied[0], ("z", "y", "aux"), axis=0, tiled=True)
+
+    names = [d for d in range(2, n_z)]
+    tied = tie(sketch, *[above[d] for d in names], *[below[d] for d in names])
+    sketch = tied[0]
+    above = dict(zip(names, tied[1:]))
+    below = dict(zip(names, tied[1 + len(names) :]))
+    third = []
+    for d in names:
+        firsts = range(1 if d == 2 else 0, n_z - d)
+        if len(firsts):
+            third += send(d, firsts)
 
     gram = lax.dot_general(sketch, sketch, (((0,), (0,)), ((), ())), precision=HIGHEST, preferred_element_type=jnp.float32)
-    hi, mid, lo = split3(sketch)
-    weighted = dot_t(lo, slab_cols) + dot_t(mid, slab_cols) + dot_t(hi, slab_cols)
-
-    projected = jnp.dot(inverse_factor(gram), weighted, precision=HIGHEST, preferred_element_type=jnp.float32)
-
-    all_rows = slab_cols.shape[0]
-    bound = jnp.maximum(largest, 1e-30) * (all_rows ** 0.5)
-    scale = 16384.0 / bound
-    sent = (projected * scale).astype(jnp.float16)
-    got = lax.all_to_all(sent, ("z", "y"), split_axis=0, concat_axis=1, tiled=True)
-    return got.astype(jnp.float32) * (bound / 16384.0)
+    tied = tie(inverse_factor(gram), sketch, *[x for _, x in third])
+    inverse, sketch = tied[:2]
+    moved += [(s, x) for (s, _), x in zip(third, tied[2:])]
+
+    arrived = [piece(z)] + [sum(x for t, x in moved if t == s) for s in range(1, n_z)]
+    arrived = rolled(jnp.stack(arrived[::-1]), n_z - 1 - z)
+    arrived = rolled(jnp.swapaxes(arrived, 0, 1), lax.rem(n_y - y, n_y))
+    slab_cols = jnp.transpose(arrived, (2, 1, 0, 3)).reshape(n_cols, n_z * n_y * rows)
+
+    weighted = sum(jnp.dot(slab_cols, part, preferred_element_type=jnp.float32) for part in split3(sketch)[::-1])
+    projected = lax.dot_general(
+        inverse, weighted, (((1,), (1,)), ((), ())), precision=HIGHEST, preferred_element_type=jnp.float32
+    )
+
+    largest = jnp.maximum(jnp.max(jnp.abs(projected)), 1e-30)
+    power = jnp.floor(14.0 - jnp.log2(largest))
+    n_more = 128 - n_cols % 128
+    more = jnp.broadcast_to(power.astype(jnp.float16), (projected.shape[0], n_more))
+    packed = jnp.concatenate([(projected * jnp.exp2(power)).astype(jnp.float16), more], axis=1)
+    packed = packed.reshape(n_z * n_y, -1, n_cols + n_more)
+    got = lax.all_to_all(packed, ("z", "y"), split_axis=0, concat_axis=0, tiled=True).astype(jnp.float32)
+    got = got[:, :, :n_cols] * jnp.exp2(-got[:, :1, n_cols : n_cols + 1])
+    return jnp.transpose(got, (1, 0, 2)).reshape(got.shape[1], -1)
 
 
 def solution(mesh):

time: 488 us -> 498 us (1.020)
  waiting for transfers between devices: 235 us -> 215 us
  other arithmetic: 6.45 us -> 23.7 us
  blocking collectives: 61.8 us -> 45.6 us
  starting transfers between devices: 27.1 us -> 40.2 us
  local copies, waits for them, and re-layouts: 23.5 us -> 34 us
  matrix products: 68.9 us -> 74.6 us
    all_to_all x2 -> x0, waiting for transfers between devices: 170 us -> none  [the longest x1 129 us: sketch_rows(): lax.all_to_all(later, ('z', 'y'), split_axis=1, concat_axis=0, tiled=True)]
    ppermute x14 -> x24, waiting for transfers between devices: 65.5 us -> 149 us  [the longest x3 61.6 us: body(): lax.ppermute(down[-1], 'z', [(i + 1, i) for i in range(n_z - s)])]
    all_gather x1, waiting for transfers between devices: 0.01 us -> 66.1 us  [body(): sketch = lax.all_gather(tied[0], ('z', 'y', 'aux'), axis=0, tiled=True)]
    unnamed x1 -> x0, blocking collectives: 61.8 us -> none
    all_to_all x0 -> x1, blocking collectives: none -> 45.6 us  [body(): lax.all_to_all(packed, ('z', 'y'), split_axis=0, concat_axis=0, tiled=True)]
    ppermute x14 -> x24, starting transfers between devices: 18.7 us -> 40.2 us  [the longest x5 10.6 us: send(): lax.ppermute(above[d], 'z', ups)]
    transpose x1 -> x4, local copies, waits for them, and re-layouts: 0.2 us -> 10.1 us  [the longest x1 6.86 us: body(): jnp.transpose(arrived, (2, 1, 0, 3)).reshape(n_cols, n_z * n_y * rows)]
    unnamed x14 -> x29, local copies, waits for them, and re-layouts: 1.27 us -> 9.88 us
  transfers between devices with their start and end apart: 17 -> 25, of which waited for: 9 -> 10; matrix products, arithmetic and copies ran while one was open for 8% -> 12% of each run, Pallas kernels for 0% -> 8%
where the time goes in v5:
time: 498 us; the launch traced here: 489 us
  waiting for transfers between devices  215 us (43%)
  matrix products  74.6 us (15%)
  blocking collectives  45.6 us (9%)
  Pallas kernels  41.2 us (8%)
  starting transfers between devices  40.2 us (8%)
  local copies, waits for them, and re-layouts  34 us (7%)
  other arithmetic  23.7 us (5%)
  between operations  15.1 us (3%)
    all_gather x1, waiting for transfers between devices, body(): sketch = lax.all_gather(tied[0], ('z', 'y', 'aux'), axis=0, tiled=True)  66.1 us
    ppermute x3, waiting for transfers between devices, body(): lax.ppermute(down[-1], 'z', [(i + 1, i) for i in range(n_z - s)])  61.6 us
    ppermute x1, waiting for transfers between devices, body(): lax.ppermute(blocks[0], 'y', [((i + k) % n_y, i) for i in range(n_y)])  50.3 us
    all_to_all x1, blocking collectives, body(): lax.all_to_all(packed, ('z', 'y'), split_axis=0, concat_axis=0, tiled=True)  45.6 us
    pallas_call x1, Pallas kernels, inverse_factor(): pl.pallas_call(inverse_factor_kernel, out_shape=jax.ShapeDtypeStruct((siz...  41.2 us
    dot_general x3, matrix products, body(): jnp.dot(slab_cols, part, preferred_element_type=jnp.float32)  22 us
    dot_general x8, matrix products, body(): jnp.dot(shard, block, preferred_element_type=jnp.float32)  21.3 us
    ppermute x5, waiting for transfers between devices, send(): lax.ppermute(above[d], 'z', ups)  21.2 us
  transfers between devices with their start and end apart: 25, of which 10 were waited for; matrix products, arithmetic and copies ran while one was open for 12% of the time, Pallas kernels for 8%

profile of v5, /device:TPU:0, one launch (start us, length us, event | category | flops | bytes accessed | tf_op | source)
XLA Modules:
  0.0 489.5 jit_solution(3451640569364810815)
XLA Ops:
  6.5 6.7 %copy.9 = bf16[256,8960]{0,1:T(8,128)(2,1)} copy(bf16[256,8960]{1,0:T(8,128)(2,1)} %param.2) | data formatting | bytes 9175040 | tf_op args[0]
  13.2 3.0 collective-permute-start
  17.5 5.7 %collective-permute-start.1 = (bf16[96,8960]{1,0:T(8,128)(2,1)S(1)}, bf16[96,8960]{1,0:T(8,128)(2,1)}, u32[]{:S(2)}, u32[]{:S(2)}) collective-permute-start(bf16[96,8960]{1,0:T(8,128)(2,1)S(1)} %bitcast.116), channel_id=1, source_target_pairs={{0,8},{8,16},{16,24},{1,9},{9,17},{17,25},{2,10},{10,18},{18,26},{... | collective-permute-start | bytes 5160968 | tf_op jit(solution)/shard_map/ppermute | solution.py:149
  23.2 33.9 %collective-permute-done.3 = bf16[96,8960]{1,0:T(8,128)(2,1)S(1)} collective-permute-done((bf16[96,8960]{1,0:T(8,128)(2,1)S(1)}, bf16[96,8960]{1,0:T(8,128)(2,1)S(1)}, u32[]{:S(2)}, u32[]{:S(2)}) %collective-permute-start.3) | collective-permute-done | bytes 1720352 | tf_op jit(solution)/shard_map/ppermute | solution.py:150
  58.4 1.9 collective-permute-start.2
  60.3 3.5 dynamic-slice_bitcast_fusion.2
  65.3 50.3 %collective-permute-done = bf16[8960,256]{1,0:T(8,128)(2,1)} collective-permute-done((bf16[8960,256]{1,0:T(8,128)(2,1)}, bf16[8960,256]{1,0:T(8,128)(2,1)}, u32[]{:S(2)}, u32[]{:S(2)}) %collective-permute-start) | collective-permute-done | bytes 4587552 | tf_op jit(solution)/shard_map/ppermute | solution.py:132
  115.5 3.4 dynamic-slice_bitcast_fusion.1
  118.9 1.6 pad_maximum_fusion
  122.6 1.6 pad_maximum_fusion.2
  124.2 3.2 fusion.38
  127.3 2.8 fusion.17
  130.2 4.2 fusion.15
  134.4 27.8 %collective-permute-done.6 = bf16[96,8960]{1,0:T(8,128)(2,1)S(1)} collective-permute-done((bf16[96,8960]{1,0:T(8,128)(2,1)}, bf16[96,8960]{1,0:T(8,128)(2,1)S(1)}, u32[]{:S(2)}, u32[]{:S(2)}) %collective-permute-start.6) | collective-permute-done | bytes 1720352 | tf_op jit(solution)/shard_map/ppermute | solution.py:150
  162.1 2.4 fusion.13
  165.5 3.2 fusion.19
  168.7 3.7 fusion.11
  173.1 2.6 collective-permute-start.13
  179.2 3.2 collective-permute-done.11
  182.4 3.9 collective-permute-start.16
  186.3 1.7 collective-permute-start.17
  188.7 4.3 collective-permute-done.9
  194.4 3.5 collective-permute-done.8
  200.6 3.5 collective-permute-done.10
  205.9 1.8 reshape.19
  209.9 1.9 reshape.20
  211.9 1.7 collective-permute-start.22
  213.6 2.8 pad_maximum_fusion.4
  216.4 66.1 %all-gather.2.cloned.1.call-done = f32[2048,768]{1,0:T(8,128)} async-done(((f32[64,768]{1,0:T(8,128)}), f32[2048,768]{1,0:T(8,128)}) %all-gather.2.cloned.1.call-update) | async-done | bytes 6291472 | tf_op jit(solution)/shard_map/all_gather | solution.py:179
  284.5 3.8 collective-permute-start.20
  288.4 1.8 collective-permute-start.21
  290.2 20.3 %fusion.39.gram_ref = f32[768,768]{1,0:T(8,128)S(1)} fusion(f32[2048,768]{1,0:T(8,128)} %all-gather.2.cloned.1.call-done), kind=kOutput, calls=%fused_computation.103 | convolution fusion | flops 14495514624 | bytes 8650752 | tf_op jit(solution)/shard_map/dot_general | solution.py:192
  310.5 41.2 %shard_map.28 = f32[768,768]{1,0:T(8,128)S(1)} custom-call(f32[768,768]{1,0:T(8,128)S(1)} %fusion.39.gram_ref), custom_call_target="tpu_custom_call" | custom-call | flops 27179089920 | bytes 4718592 | tf_op jit(solution)/shard_map/pallas_call | solution.py:99
  353.2 1.7 bitcast_dynamic-update-slice_fusion.4
  354.9 2.2 bitcast_dynamic-update-slice_fusion.2
  357.1 21.2 %collective-permute-done.23 = bf16[2,1120,256]{2,1,0:T(8,128)(2,1)S(1)} collective-permute-done((bf16[2,1120,256]{2,1,0:T(8,128)(2,1)}, bf16[2,1120,256]{2,1,0:T(8,128)(2,1)S(1)}, u32[]{:S(2)}, u32[]{:S(2)}) %collective-permute-start.23) | collective-permute-done | bytes 1146912 | tf_op jit(solution)/shard_map/ppermute | solution.py:141
  379.6 1.7 bitcast_dynamic-update-slice_fusion.5
  382.2 3.7 fusion.2
  386.0 6.9 %copy.12 = bf16[1120,4,2,256]{0,3,2,1:T(8,128)(2,1)} copy(bf16[1120,4,2,256]{3,0,2,1:T(8,128)(2,1)} %fusion.2) | data formatting | bytes 9175040 | tf_op jit(solution)/shard_map/transpose | solution.py:200
  392.8 8.3 %fusion.5 = f32[1120,768]{1,0:T(8,128)S(1)} fusion(bf16[1120,2048]{0,1:T(8,128)(2,1)} %bitcast.117, f32[2048,768]{1,0:T(8,128)} %all-gather.2.cloned.1.call-done), kind=kOutput, calls=%fused_computation.16 | convolution fusion | flops 3529506816 | bytes 14319616 | tf_op jit(solution)/shard_map/dot_general | solution.py:202
  401.2 6.8 %convolution_add_fusion.1 = f32[1120,768]{1,0:T(8,128)S(1)} fusion(f32[1120,768]{1,0:T(8,128)S(1)} %fusion.5, bf16[1120,2048]{0,1:T(8,128)(2,1)S(1)} %bitcast.118, f32[2048,768]{1,0:T(8,128)} %all-gather.2.cloned.1.call-done), kind=kOutput, calls=%fused_computation.11 | convolution fusion | flops 3531939840 | bytes 17760256 | tf_op jit(solution)/shard_map/dot_general | solution.py:202
  408.0 6.8 %convolution_add_fusion = f32[1120,768]{1,0:T(8,128)S(1)} fusion(f32[1120,768]{1,0:T(8,128)S(1)} %convolution_add_fusion.1, bf16[1120,2048]{0,1:T(8,128)(2,1)S(1)} %bitcast.119, f32[2048,768]{1,0:T(8,128)} %all-gather.2.cloned.1.call-done), kind=kOutput, calls=%fused_computation.10 | convolution fusion | flops 3527221248 | bytes 17760256 | tf_op jit(solution)/shard_map/dot_general | solution.py:202
  414.8 11.1 %abs_reduce_fusion = (f32[]{:T(128)}, f32[768,1120]{0,1:T(8,128)}) fusion(f32[768,768]{1,0:T(8,128)S(1)} %shard_map.28, f32[1120,768]{1,0:T(8,128)S(1)} %convolution_add_fusion), kind=kOutput, calls=%fused_computation.15 | convolution fusion | flops 7928954880 | bytes 9240580 | tf_op jit(solution)/shard_map/dot_general | solution.py:203
  426.6 2.3 multiply_convert_fusion
  429.0 1.6 copy.15
  431.0 45.6 %all_to_all.5 = f16[8,96,1152]{2,1,0:T(8,128)(2,1)S(1)} all-to-all(f16[8,96,1152]{2,1,0:T(8,128)(2,1)S(1)} %bitcast.114), channel_id=1, replica_groups=mesh['z'=4,'y'=2,'aux'=4] {'z','y'}, dimensions={0} | all-to-all | bytes 3538944 | tf_op jit(solution)/shard_map/all_to_all | solution.py:213
  477.4 2.1 copy.14
  479.4 2.7 reshape.23
  (82 shorter events, 26.6 us)
Async XLA Ops:
  6.5 9.7 %copy-start.1 = (bf16[8960,96]{0,1:T(8,128)(2,1)S(1)}, bf16[8960,96]{0,1:T(8,128)(2,1)}, u32[]{:S(2)}) copy-start(bf16[8960,96]{0,1:T(8,128)(2,1)} %param.3) | copy-start | bytes 5160964
  6.5 276.0 %all-gather.2.cloned.1.call-start = ((), (), s32[]{:S(2)}) async-start(), calls=%async_computation.1 | async-start | bytes 6488064 | tf_op jit(solution)/shard_map/all_gather | solution.py:179
  13.2 102.3 %collective-permute-start = (bf16[8960,256]{1,0:T(8,128)(2,1)}, bf16[8960,256]{1,0:T(8,128)(2,1)}, u32[]{:S(2)}, u32[]{:S(2)}) collective-permute-start(bf16[8960,256]{1,0:T(8,128)(2,1)} %bitcast.112), channel_id=1, source_target_pairs={{4,0},{0,4},{5,1},{1,5},{6,2},{2,6},{7,3},{3,7},{12,8},{8,12},{13,... | collective-permute-start | bytes 13762568 | tf_op jit(solution)/shard_map/ppermute | solution.py:132
  16.2 40.9 %collective-permute-start.3 = (bf16[96,8960]{1,0:T(8,128)(2,1)S(1)}, bf16[96,8960]{1,0:T(8,128)(2,1)S(1)}, u32[]{:S(2)}, u32[]{:S(2)}) collective-permute-start(bf16[96,8960]{1,0:T(8,128)(2,1)S(1)} %bitcast.115), channel_id=1, source_target_pairs={{8,0},{16,8},{24,16},{9,1},{17,9},{25,17},{10,2},{18,10},{26,18},{... | collective-permute-start | bytes 5160968 | tf_op jit(solution)/shard_map/ppermute | solution.py:150
  17.5 40.9 %collective-permute-start.1 = (bf16[96,8960]{1,0:T(8,128)(2,1)S(1)}, bf16[96,8960]{1,0:T(8,128)(2,1)}, u32[]{:S(2)}, u32[]{:S(2)}) collective-permute-start(bf16[96,8960]{1,0:T(8,128)(2,1)S(1)} %bitcast.116), channel_id=1, source_target_pairs={{0,8},{8,16},{16,24},{1,9},{9,17},{17,25},{2,10},{10,18},{18,26},{... | collective-permute-start | bytes 5160968 | tf_op jit(solution)/shard_map/ppermute | solution.py:149
  57.1 63.4 %collective-permute-start.4 = (bf16[96,8960]{1,0:T(8,128)(2,1)S(1)}, bf16[96,8960]{1,0:T(8,128)(2,1)}, u32[]{:S(2)}, u32[]{:S(2)}) collective-permute-start(bf16[96,8960]{1,0:T(8,128)(2,1)S(1)} %collective-permute-done.3), channel_id=1, source_target_pairs={{8,0},{16,8},{9,1},{17,9},{10,2},{18,10},{11,3},{19,11},{12,4},{20... | collective-permute-start | bytes 5160968 | tf_op jit(solution)/shard_map/ppermute | solution.py:150
  58.4 62.1 %collective-permute-start.2 = (bf16[96,8960]{1,0:T(8,128)(2,1)}, bf16[96,8960]{1,0:T(8,128)(2,1)}, u32[]{:S(2)}, u32[]{:S(2)}) collective-permute-start(bf16[96,8960]{1,0:T(8,128)(2,1)} %collective-permute-done.1), channel_id=1, source_target_pairs={{8,16},{16,24},{9,17},{17,25},{10,18},{18,26},{11,19},{19,27},{12,... | collective-permute-start | bytes 5160968 | tf_op jit(solution)/shard_map/ppermute | solution.py:149
  60.3 4.1 copy-start
  120.5 13.9 %collective-permute-start.5 = (bf16[96,8960]{1,0:T(8,128)(2,1)}, bf16[96,8960]{1,0:T(8,128)(2,1)S(1)}, u32[]{:S(2)}, u32[]{:S(2)}) collective-permute-start(bf16[96,8960]{1,0:T(8,128)(2,1)} %collective-permute-done.2), channel_id=1, source_target_pairs={{16,24},{17,25},{18,26},{19,27},{20,28},{21,29},{22,30},{23,31}} | collective-permute-start | bytes 5160968 | tf_op jit(solution)/shard_map/ppermute | solution.py:149
  121.3 40.8 %collective-permute-start.6 = (bf16[96,8960]{1,0:T(8,128)(2,1)}, bf16[96,8960]{1,0:T(8,128)(2,1)S(1)}, u32[]{:S(2)}, u32[]{:S(2)}) collective-permute-start(bf16[96,8960]{1,0:T(8,128)(2,1)} %collective-permute-done.4), channel_id=1, source_target_pairs={{8,0},{9,1},{10,2},{11,3},{12,4},{13,5},{14,6},{15,7}} | collective-permute-start | bytes 5160968 | tf_op jit(solution)/shard_map/ppermute | solution.py:150
  173.0 9.3 %collective-permute-start.11 = (f32[64,384]{1,0:T(8,128)S(1)}, f32[64,384]{1,0:T(8,128)S(1)}, u32[]{:S(2)}, u32[]{:S(2)}) collective-permute-start(f32[64,384]{1,0:T(8,128)S(1)} %get-tuple-element.73), channel_id=1, source_target_pairs={{0,5},{1,4},{2,7},{3,6},{4,1},{5,0},{6,3},{7,2},{8,13},{9,12},{10,... | collective-permute-start | bytes 294920 | tf_op jit(solution)/shard_map/ppermute | solution.py:168
  173.1 13.2 %collective-permute-start.13 = (f32[64,384]{1,0:T(8,128)S(1)}, f32[64,384]{1,0:T(8,128)S(1)}, u32[]{:S(2)}, u32[]{:S(2)}) collective-permute-start(f32[64,384]{1,0:T(8,128)S(1)} %get-tuple-element.74), channel_id=1, source_target_pairs={{0,7},{1,6},{2,5},{3,4},{4,3},{5,2},{6,1},{7,0},{8,15},{9,14},{10,... | collective-permute-start | bytes 294920 | tf_op jit(solution)/shard_map/ppermute | solution.py:168
  175.7 12.3 %collective-permute-start.12 = (f32[64,384]{1,0:T(8,128)S(1)}, f32[64,384]{1,0:T(8,128)S(1)}, u32[]{:S(2)}, u32[]{:S(2)}) collective-permute-start(f32[64,384]{1,0:T(8,128)S(1)} %get-tuple-element.75), channel_id=1, source_target_pairs={{0,6},{1,7},{2,4},{3,5},{4,2},{5,3},{6,0},{7,1},{8,14},{9,15},{10,... | collective-permute-start | bytes 294920 | tf_op jit(solution)/shard_map/ppermute | solution.py:168
  177.1 34.7 %collective-permute-start.14 = (bf16[2,1120,256]{2,1,0:T(8,128)(2,1)}, bf16[2,1120,256]{2,1,0:T(8,128)(2,1)S(1)}, u32[]{:S(2)}, u32[]{:S(2)}) collective-permute-start(bf16[2,1120,256]{2,1,0:T(8,128)(2,1)} %get-tuple-element.37), channel_id=1, source_target_pairs={{16,24},{17,25},{18,26},{19,27},{20,28},{21,29},{22,30},{23,31}} | collective-permute-start | bytes 3440648 | tf_op jit(solution)/shard_map/ppermute | solution.py:141
  177.9 34.0 %collective-permute-start.15 = (bf16[2,1120,256]{2,1,0:T(8,128)(2,1)}, bf16[2,1120,256]{2,1,0:T(8,128)(2,1)S(1)}, u32[]{:S(2)}, u32[]{:S(2)}) collective-permute-start(bf16[2,1120,256]{2,1,0:T(8,128)(2,1)} %get-tuple-element.38), channel_id=1, source_target_pairs={{8,0},{9,1},{10,2},{11,3},{12,4},{13,5},{14,6},{15,7}} | collective-permute-start | bytes 3440648 | tf_op jit(solution)/shard_map/ppermute | solution.py:141
  182.4 15.5 %copy-start.9 = (f32[64,384]{1,0:T(8,128)}, f32[64,384]{1,0:T(8,128)S(1)}, u32[]{:S(2)}) copy-start(f32[64,384]{1,0:T(8,128)S(1)} %collective-permute-done.11) | copy-start | bytes 294916
  182.4 29.5 %collective-permute-start.16 = (bf16[2,1120,256]{2,1,0:T(8,128)(2,1)}, bf16[2,1120,256]{2,1,0:T(8,128)(2,1)}, u32[]{:S(2)}, u32[]{:S(2)}) collective-permute-start(bf16[2,1120,256]{2,1,0:T(8,128)(2,1)} %get-tuple-element.43), channel_id=1, source_target_pairs={{0,16},{1,17},{2,18},{3,19},{4,20},{5,21},{6,22},{7,23}} | collective-permute-start | bytes 3440648 | tf_op jit(solution)/shard_map/ppermute | solution.py:141
  186.3 11.6 %copy-start.10 = (f32[64,384]{1,0:T(8,128)}, f32[64,384]{1,0:T(8,128)S(1)}, u32[]{:S(2)}) copy-start(f32[64,384]{1,0:T(8,128)S(1)} %collective-permute-done.13) | copy-start | bytes 294916
  186.3 25.5 %collective-permute-start.17 = (bf16[2,1120,256]{2,1,0:T(8,128)(2,1)}, bf16[2,1120,256]{2,1,0:T(8,128)(2,1)}, u32[]{:S(2)}, u32[]{:S(2)}) collective-permute-start(bf16[2,1120,256]{2,1,0:T(8,128)(2,1)} %get-tuple-element.44), channel_id=1, source_target_pairs={{24,8},{25,9},{26,10},{27,11},{28,12},{29,13},{30,14},{31,15}} | collective-permute-start | bytes 3440648 | tf_op jit(solution)/shard_map/ppermute | solution.py:141
  188.0 9.9 %copy-start.11 = (f32[64,384]{1,0:T(8,128)}, f32[64,384]{1,0:T(8,128)S(1)}, u32[]{:S(2)}) copy-start(f32[64,384]{1,0:T(8,128)S(1)} %collective-permute-done.12) | copy-start | bytes 294916
  188.0 5.0 %collective-permute-start.9 = (f32[64,384]{1,0:T(8,128)S(1)}, f32[64,384]{1,0:T(8,128)S(1)}, u32[]{:S(2)}, u32[]{:S(2)}) collective-permute-start(f32[64,384]{1,0:T(8,128)S(1)} %get-tuple-element.77), channel_id=1, source_target_pairs={{0,3},{1,2},{2,1},{3,0},{4,7},{5,6},{6,5},{7,4},{8,11},{9,10},{10,... | collective-permute-start | bytes 294920 | tf_op jit(solution)/shard_map/ppermute | solution.py:168
  193.0 4.9 copy-start.12
  193.0 4.9 collective-permute-start.8
  197.9 1.4 collective-permute-start.7
  199.3 4.9 collective-permute-start.10
  200.6 13.0 %copy-start.7 = (bf16[1,1120,256]{2,1,0:T(8,128)(2,1)S(1)}, bf16[1,1120,256]{2,1,0:T(8,128)(2,1)}, u32[]{:S(2)}) copy-start(bf16[1,1120,256]{2,1,0:T(8,128)(2,1)} %get-tuple-element.60) | copy-start | bytes 1720324
  200.6 13.0 %copy-start.8 = (bf16[1,1120,256]{2,1,0:T(8,128)(2,1)S(1)}, bf16[1,1120,256]{2,1,0:T(8,128)(2,1)}, u32[]{:S(2)}) copy-start(bf16[1,1120,256]{2,1,0:T(8,128)(2,1)} %get-tuple-element.61) | copy-start | bytes 1720324
  211.8 4.6 copy-start.5
  211.9 141.3 %collective-permute-start.22 = (bf16[2,1120,256]{2,1,0:T(8,128)(2,1)}, bf16[2,1120,256]{2,1,0:T(8,128)(2,1)}, u32[]{:S(2)}, u32[]{:S(2)}) collective-permute-start(bf16[2,1120,256]{2,1,0:T(8,128)(2,1)} %get-tuple-element.38), channel_id=1, source_target_pairs={{24,16},{16,8},{25,17},{17,9},{26,18},{18,10},{27,19},{19,11},{28,... | collective-permute-start | bytes 3440648 | tf_op jit(solution)/shard_map/ppermute | solution.py:141
  282.5 69.2 %collective-permute-start.18 = (bf16[2,1120,256]{2,1,0:T(8,128)(2,1)}, bf16[2,1120,256]{2,1,0:T(8,128)(2,1)S(1)}, u32[]{:S(2)}, u32[]{:S(2)}) collective-permute-start(bf16[2,1120,256]{2,1,0:T(8,128)(2,1)} %get-tuple-element.43), channel_id=1, source_target_pairs={{8,24},{9,25},{10,26},{11,27},{12,28},{13,29},{14,30},{15,31}} | collective-permute-start | bytes 3440648 | tf_op jit(solution)/shard_map/ppermute | solution.py:141
  283.2 69.9 %collective-permute-start.19 = (bf16[2,1120,256]{2,1,0:T(8,128)(2,1)}, bf16[2,1120,256]{2,1,0:T(8,128)(2,1)S(1)}, u32[]{:S(2)}, u32[]{:S(2)}) collective-permute-start(bf16[2,1120,256]{2,1,0:T(8,128)(2,1)} %get-tuple-element.44), channel_id=1, source_target_pairs={{16,0},{17,1},{18,2},{19,3},{20,4},{21,5},{22,6},{23,7}} | collective-permute-start | bytes 3440648 | tf_op jit(solution)/shard_map/ppermute | solution.py:141
  284.5 68.6 %collective-permute-start.20 = (bf16[2,1120,256]{2,1,0:T(8,128)(2,1)}, bf16[2,1120,256]{2,1,0:T(8,128)(2,1)S(1)}, u32[]{:S(2)}, u32[]{:S(2)}) collective-permute-start(bf16[2,1120,256]{2,1,0:T(8,128)(2,1)} %get-tuple-element.45), channel_id=1, source_target_pairs={{0,24},{1,25},{2,26},{3,27},{4,28},{5,29},{6,30},{7,31}} | collective-permute-start | bytes 3440648 | tf_op jit(solution)/shard_map/ppermute | solution.py:141
  288.4 64.8 %collective-permute-start.21 = (bf16[2,1120,256]{2,1,0:T(8,128)(2,1)}, bf16[2,1120,256]{2,1,0:T(8,128)(2,1)S(1)}, u32[]{:S(2)}, u32[]{:S(2)}) collective-permute-start(bf16[2,1120,256]{2,1,0:T(8,128)(2,1)} %get-tuple-element.46), channel_id=1, source_target_pairs={{24,0},{25,1},{26,2},{27,3},{28,4},{29,5},{30,6},{31,7}} | collective-permute-start | bytes 3440648 | tf_op jit(solution)/shard_map/ppermute | solution.py:141
  310.5 42.8 %copy-start.6 = (bf16[2,1120,256]{2,1,0:T(8,128)(2,1)S(1)}, bf16[2,1120,256]{2,1,0:T(8,128)(2,1)}, u32[]{:S(2)}) copy-start(bf16[2,1120,256]{2,1,0:T(8,128)(2,1)} %copy-done.5) | copy-start | bytes 3440644
  351.7 26.5 %collective-permute-start.23 = (bf16[2,1120,256]{2,1,0:T(8,128)(2,1)}, bf16[2,1120,256]{2,1,0:T(8,128)(2,1)S(1)}, u32[]{:S(2)}, u32[]{:S(2)}) collective-permute-start(bf16[2,1120,256]{2,1,0:T(8,128)(2,1)} %get-tuple-element.37), channel_id=1, source_target_pairs={{0,8},{8,16},{1,9},{9,17},{2,10},{10,18},{3,11},{11,19},{4,12},{12... | collective-permute-start | bytes 3440648 | tf_op jit(solution)/shard_map/ppermute | solution.py:141
  378.3 1.1 copy-start.2
  378.3 1.2 copy-start.3
  392.8 8.3 %copy-start.4 = (bf16[1120,4,2,256]{0,3,2,1:T(8,128)(2,1)S(1)}, bf16[1120,4,2,256]{0,3,2,1:T(8,128)(2,1)}, u32[]{:S(2)}) copy-start(bf16[1120,4,2,256]{0,3,2,1:T(8,128)(2,1)} %copy.12) | copy-start | bytes 13762564
Sparse Core Ops, SparseCore 0:
  212.0 70.4 all-gather.1
